TPU v7x, 32 devices: a whole 2x2x4 slice. The times are simulated.
32 devices in a mesh: seq: 8 (over y, x, core), head: 4 (over z).
Axes of the slice: x: 2, y: 2, z: 4, core: 2. Of those that a mesh axis runs over, the one named last changes fastest.
Arguments:
- tokens: bfloat16 [8192, 2048], P('seq'), may hold values from -6 to 6
- norm_gain: float32 [1, 2, 2048], replicated, may hold values from 0.1 to 1.9
- norm_bias: float32 [1, 2, 2048], replicated, may hold values from -1.5 to 1.5
- query_weight: bfloat16 [1, 2048, 2048], P(None, None, 'head'), may hold values from -0.125 to 0.125
- key_weight: bfloat16 [1, 2048, 2048], P(None, None, 'head'), may hold values from -0.125 to 0.125
- value_weight: bfloat16 [1, 2048, 3456], P(None, None, 'head'), may hold values from -0.125 to 0.125
- gate_weight: bfloat16 [1, 2048, 3456], P(None, None, 'head'), may hold values from -0.125 to 0.125
- output_weight: bfloat16 [1, 3456, 2048], P(None, 'head'), may hold values from -0.15625 to 0.15625
- ffn_gate: bfloat16 [1, 2048, 3456], P(None, None, 'head'), may hold values from -0.125 to 0.125
- ffn_up: bfloat16 [1, 2048, 3456], P(None, None, 'head'), may hold values from -0.125 to 0.125
- ffn_down: bfloat16 [1, 3456, 2048], P(None, 'head'), may hold values from -0.15625 to 0.15625
- grad_out: bfloat16 [8192, 2048], P('seq'), may hold values from -6 to 6
Outputs:
- result: bfloat16 [8192, 2048], P('seq')
- grad_tokens: float32 [8192, 2048], P('seq')
- grad_norm_gain: float32 [1, 2, 2048], P(None, None, 'seq')
- grad_norm_bias: float32 [1, 2, 2048], P(None, None, 'seq')
- grad_query_weight: float32 [1, 2048, 2048], P(None, 'seq', 'head')
- grad_key_weight: float32 [1, 2048, 2048], P(None, 'seq', 'head')
- grad_value_weight: float32 [1, 2048, 3456], P(None, 'seq', 'head')
- grad_gate_weight: float32 [1, 2048, 3456], P(None, 'seq', 'head')
- grad_output_weight: float32 [1, 3456, 2048], P(None, 'head', 'seq')
- grad_ffn_gate: float32 [1, 2048, 3456], P(None, 'seq', 'head')
- grad_ffn_up: float32 [1, 2048, 3456], P(None, 'seq', 'head')
- grad_ffn_down: float32 [1, 3456, 2048], P(None, 'head', 'seq')
All inputs are finite; a program needn't handle non-finite values.
Results may differ from a plain program's by a relative error of at most 0.025.
Values may be sent and summed in bfloat16 or wider, within the bound.
No kernel may reach another device: no remote copies, remote signals or barrier semaphores. Data moves between devices by JAX's collectives and lax.ppermute only.
A program may use at most 256 MiB of HBM per device.

v0:
```python
import jax
import jax.numpy as jnp
from jax import lax
from jax.sharding import PartitionSpec as P

KEY_DIM = 256
VAL_DIM = 432
LAYERS = 1


EPS = 1e-05


def prefix(shard, axis, join, neutral, backward):
    count = lax.axis_size(axis)
    place = lax.axis_index(axis)
    ahead = count - 1 - place if backward else place
    gathered = jax.tree.map(
        lambda a, kind: lax.all_gather(a.astype(kind), axis), shard, (jnp.bfloat16, jnp.bfloat16)
    )
    state = jax.tree.map(lambda a, e: jnp.zeros_like(a) + jnp.asarray(e, a.dtype), shard, neutral)

    def one(step, state):
        source = count - 1 - step if backward else step
        return join(
            state,
            jax.tree.map(
                lambda a, own: lax.dynamic_index_in_dim(a, source, 0, False).astype(own.dtype),
                gathered,
                shard,
            ),
        )

    return lax.fori_loop(0, ahead, one, state)


def layer_norm(values, gain, bias):
    mean = jnp.mean(values, axis=-1, keepdims=True)
    centred = values - mean
    spread = jnp.mean(centred * centred, axis=-1, keepdims=True)
    return centred * lax.rsqrt(spread + EPS) * gain + bias


def group_norm(values):
    mean = jnp.mean(values, axis=-1, keepdims=True)
    centred = values - mean
    spread = jnp.mean(centred * centred, axis=-1, keepdims=True)
    return centred * lax.rsqrt(spread + EPS)


def rotate(values, positions):
    half = KEY_DIM // 2
    freqs = 1.0 / 10000.0 ** jnp.linspace(0.0, 1.0, half, dtype=jnp.float32)
    angles = positions[:, None] * freqs[None, :]
    cosine = jnp.cos(angles)[:, None, :]
    sine = jnp.sin(angles)[:, None, :]
    shaped = values.reshape(values.shape[0], -1, KEY_DIM)
    first = shaped[..., :half]
    second = shaped[..., half:]
    turned = jnp.concatenate(
        [first * cosine - second * sine, second * cosine + first * sine], axis=-1
    )
    return turned.reshape(values.shape)


def matmul(left, right):
    return jnp.dot(left, right, preferred_element_type=jnp.float32)


def matmul_left(left, right):
    return lax.dot_general(
        left, right, (((0,), (0,)), ((), ())), preferred_element_type=jnp.float32
    )


def matmul_right(left, right):
    return lax.dot_general(
        left, right, (((1,), (1,)), ((), ())), preferred_element_type=jnp.float32
    )


def decay_tables(heads_here, rows):
    head_ids = (lax.axis_index("head") * heads_here).astype(jnp.float32) + jnp.arange(
        heads_here, dtype=jnp.float32
    )
    log_decay = jnp.log1p(-jnp.exp2(-5.0 - head_ids))
    offsets = jnp.arange(rows, dtype=jnp.float32)
    diff = offsets[:, None] - offsets[None, :]
    causal = diff >= 0
    within = jnp.where(
        causal[None], jnp.exp(jnp.where(causal, diff, 0.0)[None] * log_decay[:, None, None]), 0.0
    )
    query_decay = jnp.exp((offsets + 1.0)[:, None] * log_decay[None, :])
    key_decay = jnp.exp((rows - 1.0 - offsets)[:, None] * log_decay[None, :])
    block_decay = jnp.exp(rows * log_decay)
    return (rows * log_decay, within, query_decay, key_decay, block_decay)


def chain_combine(earlier, later):
    return (earlier[0] * later[1][:, None, None] + later[0], earlier[1] * later[1])


def states_before(segment_state, block_decay):
    identity = (jnp.zeros_like(segment_state), jnp.ones_like(block_decay))
    return prefix((segment_state, block_decay), "seq", chain_combine, identity, False)[0]


def states_after(local_grad, block_decay):
    identity = (jnp.zeros_like(local_grad), jnp.ones_like(block_decay))
    return prefix((local_grad, block_decay), "seq", chain_combine, identity, True)[0]


def forward_layer(inputs, gains, biases, weights, positions, tables):
    query_w, key_w, value_w, gate_w, output_w, ffn_gate_w, ffn_up_w, ffn_down_w = weights
    block_log, within, query_decay, key_decay, block_decay = tables
    rows = inputs.shape[0]
    heads_here = query_w.shape[1] // KEY_DIM
    normed_low = layer_norm(inputs, gains[0], biases[0]).astype(jnp.bfloat16)
    query_raw = matmul(normed_low, query_w)
    key_raw = matmul(normed_low, key_w)
    value_per_head = (
        matmul(normed_low, value_w).astype(jnp.bfloat16).reshape(rows, heads_here, VAL_DIM)
    )
    gate_raw = matmul(normed_low, gate_w)
    query_low = (
        (rotate(query_raw, positions) / jnp.sqrt(jnp.float32(KEY_DIM)))
        .astype(jnp.bfloat16)
        .reshape(rows, heads_here, KEY_DIM)
    )
    key_low = rotate(key_raw, positions).astype(jnp.bfloat16).reshape(rows, heads_here, KEY_DIM)
    scores = jnp.einsum("thk,shk->hts", query_low, key_low, preferred_element_type=jnp.float32)
    weights_low = (scores * within).astype(jnp.bfloat16)
    query_rescaled = (query_low.astype(jnp.float32) * query_decay[:, :, None]).astype(jnp.bfloat16)
    key_rescaled = (key_low.astype(jnp.float32) * key_decay[:, :, None]).astype(jnp.bfloat16)
    segment_state = jnp.einsum(
        "ufb,ufn->fbn", key_rescaled, value_per_head, preferred_element_type=jnp.float32
    )
    arriving_reduced = states_before(segment_state, block_decay).astype(jnp.bfloat16)
    retained = jnp.einsum(
        "hts,shv->thv", weights_low, value_per_head, preferred_element_type=jnp.float32
    )
    retained = retained + jnp.einsum(
        "gsc,scr->gsr", query_rescaled, arriving_reduced, preferred_element_type=jnp.float32
    )
    gated_low = (jax.nn.silu(gate_raw) * group_norm(retained).reshape(rows, -1)).astype(
        jnp.bfloat16
    )
    mixed = lax.psum(matmul(gated_low, output_w).astype(jnp.bfloat16), "head").astype(jnp.float32)
    middle = inputs + mixed
    ffn_in_low = layer_norm(middle, gains[1], biases[1]).astype(jnp.bfloat16)
    gate_pre = matmul(ffn_in_low, ffn_gate_w)
    up_pre = matmul(ffn_in_low, ffn_up_w)
    hidden_low = (jax.nn.gelu(gate_pre) * up_pre).astype(jnp.bfloat16)
    ffn_out = lax.psum(matmul(hidden_low, ffn_down_w).astype(jnp.bfloat16), "head").astype(
        jnp.float32
    )
    saved = (
        inputs,
        normed_low,
        query_raw,
        key_raw,
        query_low,
        key_low,
        value_per_head,
        gate_raw,
        retained,
        gated_low,
        weights_low,
        query_rescaled,
        key_rescaled,
        arriving_reduced,
        middle,
        ffn_in_low,
        gate_pre,
        up_pre,
        hidden_low,
    )
    return (middle + ffn_out, saved)


def backward_layer(grad_next, saved, gains, biases, weights, positions, tables):
    query_w, key_w, value_w, gate_w, output_w, ffn_gate_w, ffn_up_w, ffn_down_w = weights
    block_log, within, query_decay, key_decay, block_decay = tables
    (
        inputs,
        normed_low,
        query_raw,
        key_raw,
        query_low,
        key_low,
        value_per_head,
        gate_raw,
        retained,
        gated_low,
        weights_low,
        query_rescaled,
        key_rescaled,
        arriving_reduced,
        middle,
        ffn_in_low,
        gate_pre,
        up_pre,
        hidden_low,
    ) = saved
    rows = inputs.shape[0]
    grad_low = grad_next.astype(jnp.bfloat16)
    grad_down = matmul_left(hidden_low, grad_low)
    grad_hidden = matmul_right(grad_low, ffn_down_w)
    unused, pull = jax.vjp(lambda gate_in, up_in: jax.nn.gelu(gate_in) * up_in, gate_pre, up_pre)
    grad_gate_pre, grad_up_pre = pull(grad_hidden)
    gate_grad_low = grad_gate_pre.astype(jnp.bfloat16)
    up_grad_low = grad_up_pre.astype(jnp.bfloat16)
    grad_ffn_gate = matmul_left(ffn_in_low, gate_grad_low)
    grad_ffn_up = matmul_left(ffn_in_low, up_grad_low)
    ffn_part = matmul_right(gate_grad_low, ffn_gate_w) + matmul_right(up_grad_low, ffn_up_w)
    grad_ffn_in = lax.psum(ffn_part.astype(jnp.bfloat16), "head").astype(jnp.float32)
    unused, pull = jax.vjp(layer_norm, middle, gains[1], biases[1])
    grad_mid_norm, grad_gain_two, grad_bias_two = pull(grad_ffn_in)
    ffn_grads = (grad_gain_two, grad_bias_two, grad_ffn_gate, grad_ffn_up, grad_down)
    grad_middle = grad_next + grad_mid_norm
    middle_low = grad_middle.astype(jnp.bfloat16)
    grad_output = matmul_left(gated_low, middle_low)
    grad_gated = matmul_right(middle_low, output_w)
    unused, pull = jax.vjp(
        lambda gate_in, kept: jax.nn.silu(gate_in) * group_norm(kept).reshape(rows, -1),
        gate_raw,
        retained,
    )
    grad_gate_raw, grad_retained = pull(grad_gated)
    gate_raw_low = grad_gate_raw.astype(jnp.bfloat16)
    retention_reduced = grad_retained.astype(jnp.bfloat16)
    grad_incoming = jnp.einsum(
        "ufb,ufn->fbn", query_rescaled, retention_reduced, preferred_element_type=jnp.float32
    )
    gradient_local_reduced = states_after(grad_incoming, block_decay).astype(jnp.bfloat16)
    grad_scores = jnp.einsum(
        "thv,shv->hts", retention_reduced, value_per_head, preferred_element_type=jnp.float32
    )
    score_grad_low = (grad_scores * within).astype(jnp.bfloat16)
    grad_query = jnp.einsum(
        "hts,shk->thk", score_grad_low, key_low, preferred_element_type=jnp.float32
    )
    grad_query = grad_query + query_decay[:, :, None] * jnp.einsum(
        "znq,nrq->znr", retention_reduced, arriving_reduced, preferred_element_type=jnp.float32
    )
    grad_key = jnp.einsum(
        "hts,thk->shk", score_grad_low, query_low, preferred_element_type=jnp.float32
    )
    grad_key = grad_key + key_decay[:, :, None] * jnp.einsum(
        "znq,nrq->znr", value_per_head, gradient_local_reduced, preferred_element_type=jnp.float32
    )
    grad_value = jnp.einsum(
        "hts,thv->shv", weights_low, retention_reduced, preferred_element_type=jnp.float32
    )
    grad_value = grad_value + jnp.einsum(
        "gsc,scr->gsr", key_rescaled, gradient_local_reduced, preferred_element_type=jnp.float32
    )
    unused, pull = jax.vjp(
        lambda raw: rotate(raw, positions) / jnp.sqrt(jnp.float32(KEY_DIM)), query_raw
    )
    query_grad_low = pull(grad_query.reshape(rows, -1))[0].astype(jnp.bfloat16)
    unused, pull = jax.vjp(lambda raw: rotate(raw, positions), key_raw)
    key_grad_low = pull(grad_key.reshape(rows, -1))[0].astype(jnp.bfloat16)
    value_grad_low = grad_value.reshape(rows, -1).astype(jnp.bfloat16)
    grad_query_w = matmul_left(normed_low, query_grad_low)
    grad_key_w = matmul_left(normed_low, key_grad_low)
    grad_value_w = matmul_left(normed_low, value_grad_low)
    grad_gate_w = matmul_left(normed_low, gate_raw_low)
    mixer_part = matmul_right(query_grad_low, query_w) + matmul_right(key_grad_low, key_w)
    mixer_part = (
        mixer_part + matmul_right(value_grad_low, value_w) + matmul_right(gate_raw_low, gate_w)
    )
    grad_normed = lax.psum(mixer_part.astype(jnp.bfloat16), "head").astype(jnp.float32)
    unused, pull = jax.vjp(layer_norm, inputs, gains[0], biases[0])
    grad_in_norm, grad_gain_one, grad_bias_one = pull(grad_normed)
    grad_inputs = grad_middle + grad_in_norm
    mixer_grads = (
        grad_gain_one,
        grad_bias_one,
        grad_query_w,
        grad_key_w,
        grad_value_w,
        grad_gate_w,
        grad_output,
    )
    grads = (
        jnp.stack([mixer_grads[0], ffn_grads[0]]),
        jnp.stack([mixer_grads[1], ffn_grads[1]]),
        mixer_grads[2],
        mixer_grads[3],
        mixer_grads[4],
        mixer_grads[5],
        mixer_grads[6],
        ffn_grads[2],
        ffn_grads[3],
        ffn_grads[4],
    )
    return (grad_inputs, grads)


def on_device(
    tokens,
    norm_gain,
    norm_bias,
    query_weight,
    key_weight,
    value_weight,
    gate_weight,
    output_weight,
    ffn_gate,
    ffn_up,
    ffn_down,
    grad_out,
):
    rows = tokens.shape[0]
    heads_here = query_weight.shape[2] // KEY_DIM
    positions = (lax.axis_index("seq") * rows + jnp.arange(rows, dtype=jnp.int32)).astype(
        jnp.float32
    )
    tables = decay_tables(heads_here, rows)
    current = tokens.astype(jnp.float32)
    layer_index = 0
    weights = (
        query_weight[layer_index],
        key_weight[layer_index],
        value_weight[layer_index],
        gate_weight[layer_index],
        output_weight[layer_index],
        ffn_gate[layer_index],
        ffn_up[layer_index],
        ffn_down[layer_index],
    )
    current, saved = forward_layer(
        current, norm_gain[layer_index], norm_bias[layer_index], weights, positions, tables
    )
    kept = [saved]
    outcome = current.astype(jnp.bfloat16)
    grad_current = grad_out.astype(jnp.float32)
    layer_results = [None] * LAYERS
    for layer_index in reversed(range(LAYERS)):
        weights = (
            query_weight[layer_index],
            key_weight[layer_index],
            value_weight[layer_index],
            gate_weight[layer_index],
            output_weight[layer_index],
            ffn_gate[layer_index],
            ffn_up[layer_index],
            ffn_down[layer_index],
        )
        grad_current, grads = backward_layer(
            grad_current,
            kept[layer_index],
            norm_gain[layer_index],
            norm_bias[layer_index],
            weights,
            positions,
            tables,
        )
        layer_results[layer_index] = grads
    stacked = tuple((jnp.stack([layer_results[0][member]]) for member in range(10)))
    stacked = (
        lax.psum_scatter(
            stacked[0].astype(jnp.bfloat16), "seq", scatter_dimension=2, tiled=True
        ).astype(jnp.float32),
        lax.psum_scatter(
            stacked[1].astype(jnp.bfloat16), "seq", scatter_dimension=2, tiled=True
        ).astype(jnp.float32),
        lax.psum_scatter(
            stacked[2].astype(jnp.bfloat16), "seq", scatter_dimension=1, tiled=True
        ).astype(jnp.float32),
        lax.psum_scatter(
            stacked[3].astype(jnp.bfloat16), "seq", scatter_dimension=1, tiled=True
        ).astype(jnp.float32),
        lax.psum_scatter(
            stacked[4].astype(jnp.bfloat16), "seq", scatter_dimension=1, tiled=True
        ).astype(jnp.float32),
        lax.psum_scatter(
            stacked[5].astype(jnp.bfloat16), "seq", scatter_dimension=1, tiled=True
        ).astype(jnp.float32),
        lax.psum_scatter(
            stacked[6].astype(jnp.bfloat16), "seq", scatter_dimension=2, tiled=True
        ).astype(jnp.float32),
        lax.psum_scatter(
            stacked[7].astype(jnp.bfloat16), "seq", scatter_dimension=1, tiled=True
        ).astype(jnp.float32),
        lax.psum_scatter(
            stacked[8].astype(jnp.bfloat16), "seq", scatter_dimension=1, tiled=True
        ).astype(jnp.float32),
        lax.psum_scatter(
            stacked[9].astype(jnp.bfloat16), "seq", scatter_dimension=2, tiled=True
        ).astype(jnp.float32),
    )
    return (
        outcome,
        grad_current,
        stacked[0],
        stacked[1],
        stacked[2],
        stacked[3],
        stacked[4],
        stacked[5],
        stacked[6],
        stacked[7],
        stacked[8],
        stacked[9],
    )


def solution(mesh):
    return jax.shard_map(
        on_device,
        mesh=mesh,
        in_specs=(
            P("seq", None),
            P(),
            P(),
            P(None, None, "head"),
            P(None, None, "head"),
            P(None, None, "head"),
            P(None, None, "head"),
            P(None, "head", None),
            P(None, None, "head"),
            P(None, None, "head"),
            P(None, "head", None),
            P("seq", None),
        ),
        out_specs=(
            P("seq", None),
            P("seq", None),
            P(None, None, "seq"),
            P(None, None, "seq"),
            P(None, "seq", "head"),
            P(None, "seq", "head"),
            P(None, "seq", "head"),
            P(None, "seq", "head"),
            P(None, "head", "seq"),
            P(None, "seq", "head"),
            P(None, "seq", "head"),
            P(None, "head", "seq"),
        ),
        check_vma=False,
    )
```

profile of v0, /device:TPU:0, one launch (start us, length us, event | category | flops | bytes accessed | tf_op | source)
XLA Modules:
  0.0 1368.0 jit_solution(4094271297382865919)
XLA Ops:
  15.7 3.9 copy.69
  19.6 4.0 copy.68
  33.0 3.9 fusion.68
  43.7 10.7 all-gather.2
  63.8 3.8 fusion.86
  67.6 12.8 all-gather.6.cloned.1.call-done
  89.9 6.1 fusion.48
  97.3 6.2 convolution_convert_fusion.1
  103.5 204.6 %all-reduce.9.cloned.1.call-done = bf16[1024,2048]{1,0:T(8,128)(2,1)} async-done(((bf16[1024,2048]{1,0:T(8,128)(2,1)}), bf16[1024,2048]{1,0:T(8,128)(2,1)}) %all-reduce.9.cloned.1.call-update) | async-done | bytes 4194320 | tf_op jit(solution)/shard_map/psum | solution.py:148
  308.1 4.8 fusion.16
  319.1 3.9 fusion.39
  323.1 3.9 fusion.43
  327.0 7.8 multiply_convert_fusion.2
  334.8 4.6 fusion.41
  339.5 6.5 add_convert_fusion.1
  346.1 154.1 %all-reduce.11.cloned.1.call-done = bf16[1024,2048]{1,0:T(8,128)(2,1)} async-done(((bf16[1024,2048]{1,0:T(8,128)(2,1)}), bf16[1024,2048]{1,0:T(8,128)(2,1)}) %all-reduce.11.cloned.1.call-update) | async-done | bytes 4194320 | tf_op jit(solution)/shard_map/psum | solution.py:216
  500.2 8.4 fusion.11
  508.7 3.9 fusion.83
  512.6 8.2 fusion.18
  520.8 11.5 fusion.72
  538.4 8.4 convert_bitcast_fusion.1
  546.8 8.3 convert_bitcast_fusion.2
  555.2 8.3 convert_bitcast_fusion
  563.5 8.4 convert_bitcast_fusion.3
  572.2 4.0 fusion.76
  576.1 6.7 convert_bitcast_fusion.4
  583.6 7.7 multiply_convert_fusion
  597.0 50.3 %while.27 = (s32[]{:T(128)}, f32[2,256,432]{2,1,0:T(8,128)}, s32[]{:T(128)}, bf16[8,2]{1,0:T(8,128)(2,1)}, bf16[8,2,256,432]{2,3,1,0:T(8,128)(2,1)}, /*index=5*/s32[]{:T(128)}, s32[]{:T(128)}, s32[]{:T(128)}, s32[]{:T(128)}) while((s32[]{:T(128)}, f32[2,256,432]{2,1,0:T(8,128)}, s32[]{:T(128)}, bf16[8,2]{1,0:T(8,128)(2,1)}, ...), condition=%wide.region_16.18_spmd, body=%wide.region_15.17_spmd.sunk | while | flops 663560 | bytes 3981487 | solution.py:34
  656.7 3.8 fusion.59
  663.2 6.0 fusion.60
  669.3 4.9 fusion.87
  677.1 5.3 convert_bitcast_fusion.5
  682.9 7.8 convolution_convert_fusion
  690.6 6.8 fusion.53
  697.5 5.7 fusion.66
  703.2 6.9 fusion.49
  710.0 13.2 add_convert_fusion
  733.6 43.5 %reduce-scatter.23.cloned.1.call-done = bf16[1,864,256]{2,1,0:T(8,128)(2,1)} async-done(((bf16[1,864,2048]{2,1,0:T(8,128)(2,1)}), bf16[1,864,256]{2,1,0:T(8,128)(2,1)}) %reduce-scatter.23.cloned.1.call-update) | async-done | bytes 442384 | tf_op jit(solution)/shard_map/reduce_scatter | solution.py:381
  779.1 49.6 %reduce-scatter.21.cloned.1.call-done = bf16[1,256,864]{1,2,0:T(8,128)(2,1)} async-done(((bf16[1,2048,864]{1,2,0:T(8,128)(2,1)}), bf16[1,256,864]{1,2,0:T(8,128)(2,1)}) %reduce-scatter.21.cloned.1.call-update) | async-done | bytes 442384 | tf_op jit(solution)/shard_map/reduce_scatter | solution.py:378
  830.7 42.4 %reduce-scatter.15.cloned.1.call-done = bf16[1,256,512]{2,1,0:T(8,128)(2,1)} async-done(((bf16[1,2048,512]{2,1,0:T(8,128)(2,1)}), bf16[1,256,512]{2,1,0:T(8,128)(2,1)}) %reduce-scatter.15.cloned.1.call-update) | async-done | bytes 262160 | tf_op jit(solution)/shard_map/reduce_scatter | solution.py:369
  874.9 43.1 %reduce-scatter.17.cloned.1.call-done = bf16[1,256,512]{2,1,0:T(8,128)(2,1)} async-done(((bf16[1,2048,512]{2,1,0:T(8,128)(2,1)}), bf16[1,256,512]{2,1,0:T(8,128)(2,1)}) %reduce-scatter.17.cloned.1.call-update) | async-done | bytes 262160 | tf_op jit(solution)/shard_map/reduce_scatter | solution.py:372
  919.8 49.6 %reduce-scatter.19.cloned.1.call-done = bf16[1,256,864]{1,2,0:T(8,128)(2,1)} async-done(((bf16[1,2048,864]{1,2,0:T(8,128)(2,1)}), bf16[1,256,864]{1,2,0:T(8,128)(2,1)}) %reduce-scatter.19.cloned.1.call-update) | async-done | bytes 442384 | tf_op jit(solution)/shard_map/reduce_scatter | solution.py:375
  971.4 292.7 %all-reduce.13.cloned.1.call-done = (bf16[1024,2048]{1,0:T(8,128)(2,1)}, bf16[1024,2048]{1,0:T(8,128)(2,1)}) async-done(((bf16[1024,2048]{1,0:T(8,128)(2,1)}, bf16[1024,2048]{1,0:T(8,128)(2,1)}), (bf16[1024,2048]{1,0:T(8,128)(2,1)}, bf16[1024,2048]{1,0:T(8,128)(2,1)})) %all-reduce.13.cloned.1.call-update) | async-done | bytes 8388624 | tf_op jit(solution)/shard_map/psum | solution.py:154
  1264.1 5.1 fusion.14
  1274.6 6.3 fusion.12
  1294.2 16.6 %add_add_fusion.2 = (f32[1024,2048]{1,0:T(8,128)}, bf16[1024,2048]{1,0:T(8,128)(2,1)}) fusion(bf16[1024,2048]{1,0:T(8,128)(2,1)} %param.18, bf16[1024,2048]{1,0:T(8,128)(2,1)} %get-tuple-element.188, f32[1024,2048]{1,0:T(8,128)} %copy-done.8, bf16[1024,2048]{1,0:T(8,128)(2,1)} %param.29, f32[1024]{0:T(1024)} %negate_multiply_fusion.1, f32[1024]{0:T(1024)} %copy-done.72, ...), kind=kLoop, calls=%fused_computation.30 | loop fusion | flops 37748736 | bytes 41971712 | tf_op jit(solution)/shard_map/add | solution.py:276
  1310.8 10.0 reduce-scatter.31.cloned.1.call-done
  1323.9 34.2 %reduce-scatter.33.cloned.1.call-done = bf16[256,2]{1,0:T(8,128)(2,1)} async-done(((bf16[2048,2]{1,0:T(8,128)(2,1)}), bf16[256,2]{1,0:T(8,128)(2,1)}) %reduce-scatter.33.cloned.1.call-update) | async-done | bytes 1040
  (340 shorter events, 173.8 us)
Async XLA Ops:
  7.2 319.8 %copy-start = (bf16[1,864,2048]{2,1,0:T(8,128)(2,1)S(1)}, bf16[1,864,2048]{2,1,0:T(8,128)(2,1)}, u32[]{:S(2)}) copy-start(bf16[1,864,2048]{2,1,0:T(8,128)(2,1)} %param.28) | copy-start | bytes 10616836
  7.2 73.2 %all-gather.6.cloned.1.call-start = ((), (), s32[]{:S(2)}) async-start(), calls=%async_computation.20 | async-start | bytes 3981312 | tf_op jit(solution)/shard_map/all_gather | solution.py:19
  12.6 11.0 copy-start.54
  14.5 9.1 copy-start.66
  15.1 8.5 copy-start.52
  33.0 5.9 copy-start.79
  33.0 5.9 copy-start.80
  33.0 5.9 copy-start.83
  43.6 264.5 %all-reduce.9.cloned.1.call-start = ((), (), s32[]{:S(2)}) async-start(), calls=%async_computation.10 | async-start | bytes 8388608 | tf_op jit(solution)/shard_map/psum | solution.py:148
  89.9 6.1 copy-start.41
  89.9 7.3 copy-start.88
  103.4 396.7 %all-reduce.11.cloned.1.call-start = ((), (), s32[]{:S(2)}) async-start(), calls=%async_computation.11 | async-start | bytes 8388608 | tf_op jit(solution)/shard_map/psum | solution.py:216
  308.1 5.9 copy-start.4
  346.0 249.9 %all-gather.8.cloned.1.call-start = ((), (), s32[]{:S(2)}) async-start(), calls=%async_computation.21 | async-start | bytes 3981312 | tf_op jit(solution)/shard_map/all_gather | solution.py:19
  500.1 8.5 copy-start.71
  500.2 8.5 copy-start.3
  500.2 8.5 copy-start.5
  500.2 8.5 copy-start.10
  500.2 8.5 copy-start.61
  500.2 8.5 copy-start.63
  500.2 8.5 copy-start.69
  512.6 8.3 copy-start.8
  512.6 8.3 copy-start.73
  520.8 11.5 copy-start.7
  537.9 189.7 %reduce-scatter.27.cloned.1.call-start = ((), (), s32[]{:S(2)}) async-start(), calls=%async_computation.18 | async-start | bytes 3981312 | tf_op jit(solution)/shard_map/reduce_scatter | solution.py:387
  546.8 182.8 %reduce-scatter.25.cloned.1.call-start = ((), (), s32[]{:S(2)}) async-start(), calls=%async_computation.17 | async-start | bytes 3981312 | tf_op jit(solution)/shard_map/reduce_scatter | solution.py:384
  555.1 176.5 %reduce-scatter.29.cloned.1.call-start = ((), (), s32[]{:S(2)}) async-start(), calls=%async_computation.19 | async-start | bytes 3981312 | tf_op jit(solution)/shard_map/reduce_scatter | solution.py:390
  563.5 213.6 %reduce-scatter.23.cloned.1.call-start = ((), (), s32[]{:S(2)}) async-start(), calls=%async_computation.16 | async-start | bytes 3981312 | tf_op jit(solution)/shard_map/reduce_scatter | solution.py:381
  571.9 256.8 %reduce-scatter.21.cloned.1.call-start = ((), (), s32[]{:S(2)}) async-start(), calls=%async_computation.15 | async-start | bytes 3981312 | tf_op jit(solution)/shard_map/reduce_scatter | solution.py:378
  582.9 290.2 %reduce-scatter.15.cloned.1.call-start = ((), (), s32[]{:S(2)}) async-start(), calls=%async_computation.12 | async-start | bytes 2359296 | tf_op jit(solution)/shard_map/reduce_scatter | solution.py:369
  583.5 9.7 copy-start.17
  583.5 9.7 copy-start.22
  583.5 9.7 copy-start.26
  660.5 257.5 %reduce-scatter.17.cloned.1.call-start = ((), (), s32[]{:S(2)}) async-start(), calls=%async_computation.13 | async-start | bytes 2359296 | tf_op jit(solution)/shard_map/reduce_scatter | solution.py:372
  669.2 300.2 %reduce-scatter.19.cloned.1.call-start = ((), (), s32[]{:S(2)}) async-start(), calls=%async_computation.14 | async-start | bytes 3981312 | tf_op jit(solution)/shard_map/reduce_scatter | solution.py:375
  682.4 581.8 %all-reduce.13.cloned.1.call-start = ((), (), s32[]{:S(2)}) async-start(), calls=%async_computation.24 | async-start | bytes 16777216 | tf_op jit(solution)/shard_map/psum | solution.py:154
  682.8 7.8 copy-start.90
  682.9 7.8 copy-start.94
  690.6 6.8 copy-start.42
  690.6 6.8 copy-start.50
  703.1 6.9 copy-start.16
  703.2 6.9 copy-start.33
  723.3 597.5 %reduce-scatter.31.cloned.1.call-start = ((), (), s32[]{:S(2)}) async-start(), calls=%async_computation.22 | async-start | bytes 589824
  731.6 532.6 %copy-start.53 = (f32[1,1,2048]{2,1,0:T(1,128)S(1)}, f32[1,1,2048]{2,1,0:T(1,128)}, u32[]{:S(2)}) copy-start(f32[1,1,2048]{2,1,0:T(1,128)} %copy-done.52) | copy-start | bytes 24580
  731.6 532.6 %copy-start.55 = (f32[1024]{0:T(1024)S(1)}, f32[1024]{0:T(1024)}, u32[]{:S(2)}) copy-start(f32[1024]{0:T(1024)} %copy-done.54) | copy-start | bytes 12292
  1273.4 7.6 copy-start.72
  1274.6 6.9 copy-start.75
  1287.5 70.7 %reduce-scatter.33.cloned.1.call-start = ((), (), s32[]{:S(2)}) async-start(), calls=%async_computation.23 | async-start | bytes 589824
  (66 other events, 202.1 us)
Sparse Core Ops, SparseCore 0:
  43.7 36.6 all-gather.5
  103.6 204.5 all-reduce.8
  346.1 153.9 all-reduce.10
  538.0 32.9 all-gather.7
  574.4 48.0 reduce-scatter.26
  625.8 48.0 reduce-scatter.24
  677.4 48.0 reduce-scatter.28
  729.0 48.0 reduce-scatter.22
  780.6 48.0 reduce-scatter.20
  831.8 41.1 reduce-scatter.14
  876.7 41.2 reduce-scatter.16
  921.3 48.0 reduce-scatter.18
  972.6 291.5 all-reduce.12
  1287.6 33.1 reduce-scatter.30
  1324.0 34.1 reduce-scatter.32
where the time goes:
time: 1370 us
  waiting for transfers between devices  937 us (68%)
  matrix products  193 us (14%)
  other arithmetic  133 us (10%)
  local copies, waits for them, and re-layouts  76.4 us (6%)
  between operations  15.3 us (1%)
    psum x1, waiting for transfers between devices, forward_layer(): lax.psum(matmul(hidden_low, ffn_down_w).astype(jnp.bfloat16), 'head')  293 us
    psum x1, waiting for transfers between devices, forward_layer(): lax.psum(matmul(gated_low, output_w).astype(jnp.bfloat16), 'head')  205 us
    psum x1, waiting for transfers between devices, backward_layer(): lax.psum(ffn_part.astype(jnp.bfloat16), 'head').astype(jnp.float32)  154 us
    dot_general x8, matrix products, matmul_right(): lax.dot_general(left, right, (((1,), (1,)), ((), ())), preferred_element_...  63 us
    dot_general x8, matrix products, matmul_left(): lax.dot_general(left, right, (((0,), (0,)), ((), ())), preferred_element_...  55.1 us
    reduce_scatter x1, waiting for transfers between devices, on_device(): lax.psum_scatter(stacked[4].astype(jnp.bfloat16), 'seq', scatter_dimensio...  49.6 us
    reduce_scatter x1, waiting for transfers between devices, on_device(): lax.psum_scatter(stacked[5].astype(jnp.bfloat16), 'seq', scatter_dimensio...  49.6 us
    unnamed x17, waiting for transfers between devices  44.5 us
  transfers between devices with their start and end apart: 15, of which 11 were waited for; matrix products, arithmetic and copies ran while one was open for 17% of the time, Pallas kernels for 0%

commit v1 on v0

v1 whole, which is shorter than its diff:
```python
import jax
import jax.numpy as jnp
from jax import lax
from jax.experimental import pallas as pl
from jax.experimental.pallas import tpu as pltpu
from jax.sharding import PartitionSpec as P

KEY_DIM = 256
VAL_DIM = 432
EPS = 1e-05
CHUNKS = 4


def matmul(left, right):
    return jnp.dot(left, right, preferred_element_type=jnp.float32)


def matmul_left(left, right):
    return lax.dot_general(
        left, right, (((0,), (0,)), ((), ())), preferred_element_type=jnp.float32
    )


def matmul_right(left, right):
    return lax.dot_general(
        left, right, (((1,), (1,)), ((), ())), preferred_element_type=jnp.float32
    )


def low(values):
    return values.astype(jnp.bfloat16)


def wide(values):
    return values.astype(jnp.float32)


ANY = pl.BlockSpec(memory_space=pl.ANY)
SMEM = pl.BlockSpec(memory_space=pltpu.SMEM)
VMEM = pl.BlockSpec(memory_space=pltpu.VMEM)
EXTRA_ROWS = 32


def params(mebibytes):
    return pltpu.CompilerParams(vmem_limit_bytes=mebibytes * 2**20)


def small_cost():
    return pl.CostEstimate(flops=0, bytes_accessed=1_000_000, transcendentals=0)


def struct(shape, dtype):
    return jax.ShapeDtypeStruct(tuple(shape), dtype)


def in_hbm(shape, dtype=jnp.bfloat16):
    return pltpu.HBM(tuple(shape), dtype)


def pin(values):
    return pltpu.with_memory_space_constraint(values, pltpu.HBM)


def vmem(shape, dtype=jnp.bfloat16):
    return pltpu.VMEM(tuple(shape), dtype)


def fetch(source, target, sem):
    copy = pltpu.make_async_copy(source, target, sem)
    copy.start()
    return copy


def tiles(rows, body, size=256):
    for start in range(0, rows, size):
        body(pl.ds(start, min(size, rows - start)))


def row_mean(values):
    return jnp.mean(values, axis=-1, keepdims=True)


def norm_back(grad, unit, scale):
    return scale * (grad - row_mean(grad) - unit * row_mean(grad * unit))


def norm_parts(values):
    mean = row_mean(values)
    centred = values - mean
    scale = lax.rsqrt(row_mean(centred * centred) + EPS)
    return centred * scale, mean, scale


def spread_lanes(column):
    return jnp.broadcast_to(column, (column.shape[0], 128))


def turn(values, cosine, sine):
    half = KEY_DIM // 2
    parts = []
    for start in range(0, values.shape[1], KEY_DIM):
        first = values[:, start : start + half]
        second = values[:, start + half : start + KEY_DIM]
        parts += [first * cosine - second * sine, second * cosine + first * sine]
    return jnp.concatenate(parts, axis=1)


def decay_rows(log_decay, first, rows, sign):
    row = lax.broadcasted_iota(jnp.int32, (rows, KEY_DIM), 0).astype(jnp.float32)
    return jnp.exp((first + sign * row) * log_decay)


def decay_square(log_decay, apart, size):
    t = lax.broadcasted_iota(jnp.int32, (size, size), 0)
    s = lax.broadcasted_iota(jnp.int32, (size, size), 1)
    gap = apart + t - s
    table = jnp.exp(jnp.maximum(gap, 0).astype(jnp.float32) * log_decay)
    return jnp.where(gap >= 0, table, 0.0) if apart == 0 else table


def add_call(held, came):
    rows, cols = held.shape

    def kernel(held, came, out):
        out[...] = (wide(held[...]) + wide(came[...])).astype(out.dtype)

    spec = pl.BlockSpec((rows // 2, cols), lambda i: (i, 0))
    return pl.pallas_call(
        kernel,
        grid=(2,),
        in_specs=[spec, spec],
        out_specs=spec,
        out_shape=struct(held.shape, held.dtype),
        compiler_params=params(8),
        cost_estimate=small_cost(),
    )(held, came)


def first_call(decay, tok, gain, bias, cos, sin, key_w, value_w):
    rows, width = tok.shape
    keys, values = key_w.shape[1], value_w.shape[0]
    heads = keys // KEY_DIM
    size = rows // CHUNKS

    def kernel(decay, tok, gain, bias, cos, sin, key_w, value_w, normed, mean_out, scale_out, key, value, state, tok_v, key_v, value_v, normed_v, product, sems):
        span = lambda i: pl.ds(i * size, size)
        loads = [fetch(tok.at[span(i)], tok_v.at[span(i)], sems.at[i]) for i in range(CHUNKS)]
        load_key = fetch(key_w, key_v, sems.at[CHUNKS])
        load_value = fetch(value_w, value_v, sems.at[CHUNKS + 1])
        stores = []
        for i in range(CHUNKS):
            loads[i].wait()

            def norm(part):
                unit, mean, scale = norm_parts(wide(tok_v[part]))
                normed_v[part] = low(unit * gain[0:1] + bias[0:1])
                mean_out[part] = spread_lanes(mean)
                scale_out[part] = spread_lanes(scale)

            norm(span(i))
            stores.append(fetch(normed_v.at[span(i)], normed.at[span(i)], sems.at[CHUNKS + 2 + i]))
        load_key.wait()
        product[...] = matmul(normed_v[...], key_v[...])

        def rotate(part):
            key[part] = low(turn(product[part], cos[part], sin[part]))

        tiles(rows, rotate)
        load_value.wait()
        value[...] = low(matmul_right(value_v[...], normed_v[...]))
        for head in range(heads):
            k = wide(key[:, head * KEY_DIM : (head + 1) * KEY_DIM])
            scaled = low(k * decay_rows(decay[head], rows - 1.0, rows, -1.0))
            v = value[head * VAL_DIM : (head + 1) * VAL_DIM]
            state[head] = low(matmul(v, scaled))
        for store in stores:
            store.wait()

    return pl.pallas_call(
        kernel,
        in_specs=[SMEM, ANY, VMEM, VMEM, VMEM, VMEM, ANY, ANY],
        out_specs=[ANY] + [VMEM] * 5,
        out_shape=[
            in_hbm((rows, width)),
            in_hbm((rows, 128), jnp.float32),
            in_hbm((rows, 128), jnp.float32),
            in_hbm((rows, keys)),
            in_hbm((values, rows)),
            struct((heads, VAL_DIM, KEY_DIM), jnp.bfloat16),
        ],
        scratch_shapes=[
            vmem((rows, width)),
            vmem(key_w.shape),
            vmem(value_w.shape),
            vmem((rows, width)),
            vmem((rows, keys), jnp.float32),
            pltpu.SemaphoreType.DMA((2 * CHUNKS + 2,)),
        ],
        compiler_params=params(50),
        cost_estimate=small_cost(),
    )(decay, pin(tok), gain, bias, cos, sin, pin(key_w), pin(value_w))


def second_call(place, normed, cos, sin, query_w, gate_w):
    rows, width = normed.shape
    keys, values = query_w.shape[1], gate_w.shape[0]
    count = place.shape[0] - 1
    block = width // count

    def kernel(place, normed, cos, sin, query_w, gate_w, query, gate, arranged, normed_v, query_v, gate_v, product, sems):
        load = fetch(normed, normed_v, sems.at[0])
        load_query = fetch(query_w, query_v, sems.at[1])
        load_gate = fetch(gate_w, gate_v, sems.at[2])
        load.wait()
        stores = []
        for b in range(count):
            start = pl.multiple_of(place[1 + b] * block, block)
            source = normed_v.at[:, pl.ds(b * block, block)]
            stores.append(fetch(source, arranged.at[:, pl.ds(start, block)], sems.at[3 + b]))
        load_query.wait()
        product[...] = matmul(normed_v[...], query_v[...])

        def rotate(part):
            turned = turn(product[part], cos[part], sin[part])
            query[part] = low(turned * (1.0 / KEY_DIM**0.5))

        tiles(rows, rotate)
        load_gate.wait()
        gate[...] = low(matmul_right(gate_v[...], normed_v[...]))
        for store in stores:
            store.wait()

    return pl.pallas_call(
        kernel,
        in_specs=[SMEM, ANY, VMEM, VMEM, ANY, ANY],
        out_specs=[VMEM, VMEM, ANY],
        out_shape=[in_hbm((rows, keys)), in_hbm((values, rows)), in_hbm((rows, width))],
        scratch_shapes=[
            vmem((rows, width)),
            vmem(query_w.shape),
            vmem(gate_w.shape),
            vmem((rows, keys), jnp.float32),
            pltpu.SemaphoreType.DMA((3 + count,)),
        ],
        compiler_params=params(44),
        cost_estimate=small_cost(),
    )(place, pin(normed), cos, sin, pin(query_w), pin(gate_w))


def intra_call(decay, query, key, value):
    rows = query.shape[0]
    heads = query.shape[1] // KEY_DIM
    size = rows // CHUNKS

    def kernel(decay, query, key, value, intra):
        span = lambda i: slice(i * size, (i + 1) * size)
        rate = decay[pl.program_id(0)]
        tables = [decay_square(rate, d * size, size) for d in range(CHUNKS)]
        for i in range(CHUNKS):
            q = query[span(i)]
            weights = [
                low(matmul_right(q, key[span(j)]) * tables[i - j]) for j in range(i + 1)
            ]
            weights = jnp.concatenate(weights, axis=1) if i else weights[0]
            intra[:, span(i)] = matmul_right(value[:, : (i + 1) * size], weights)

    column = pl.BlockSpec((rows, KEY_DIM), lambda h: (0, h))
    per_head = pl.BlockSpec((VAL_DIM, rows), lambda h: (h, 0))
    return pl.pallas_call(
        kernel,
        grid=(heads,),
        in_specs=[SMEM, column, column, per_head],
        out_specs=per_head,
        out_shape=in_hbm((heads * VAL_DIM, rows), jnp.float32),
        compiler_params=params(44),
        cost_estimate=small_cost(),
    )(decay, pin(query), pin(key), pin(value))


def mix_call(index, decay, query, gate, intra, state, output_w, buffers):
    rows, keys = query.shape
    values, width = output_w.shape
    heads = keys // KEY_DIM
    size = rows // CHUNKS
    first = buffers is None

    def kernel(decay, query, gate, intra, state, output_w, *refs):
        refs = refs if first else refs[2:]
        part, scale_out, gated, units = refs[:4]
        query_v, gate_v, intra_v, weight, gated_v, unit_v, sems = refs[4:]
        here = pl.ds(index * size, size)
        loads = [
            fetch(query.at[here], query_v, sems.at[0]),
            fetch(intra.at[:, here], intra_v, sems.at[1]),
            fetch(gate.at[:, here], gate_v, sems.at[2]),
        ]
        load_weight = fetch(output_w, weight, sems.at[3])
        for load in loads:
            load.wait()
        for head in range(heads):
            span = slice(head * VAL_DIM, (head + 1) * VAL_DIM)
            q = wide(query_v[:, head * KEY_DIM : (head + 1) * KEY_DIM])
            scaled = low(q * decay_rows(decay[head], index * size + 1.0, size, 1.0))
            o = intra_v[span] + matmul_right(state[head], scaled)
            centred = o - jnp.mean(o, axis=0, keepdims=True)
            scale = lax.rsqrt(jnp.mean(centred * centred, axis=0, keepdims=True) + EPS)
            unit = centred * scale
            unit_v[span] = low(unit)
            scale_out[head] = jnp.broadcast_to(scale, (8, size))
            g = wide(gate_v[span])
            gated_v[span] = low(g * jax.nn.sigmoid(g) * unit)
        stores = [
            fetch(gated_v, gated.at[:, here], sems.at[4]),
            fetch(unit_v, units.at[:, here], sems.at[5]),
        ]
        load_weight.wait()
        part[...] = low(matmul_left(gated_v[...], weight[...]))
        for store in stores:
            store.wait()

    return pl.pallas_call(
        kernel,
        in_specs=[SMEM, ANY, ANY, ANY, VMEM, ANY] + [ANY] * (0 if first else 2),
        out_specs=[VMEM, VMEM, ANY, ANY],
        out_shape=[
            struct((size, width), jnp.bfloat16),
            in_hbm((heads, 8, size), jnp.float32),
            in_hbm((values, rows)),
            in_hbm((values, rows)),
        ],
        scratch_shapes=[
            vmem((size, keys)),
            vmem((values, size)),
            vmem((values, size), jnp.float32),
            vmem(output_w.shape),
            vmem((values, size)),
            vmem((values, size)),
            pltpu.SemaphoreType.DMA((6,)),
        ],
        input_output_aliases={} if first else {6: 2, 7: 3},
        compiler_params=params(20),
        cost_estimate=small_cost(),
    )(decay, pin(query), pin(gate), pin(intra), state, pin(output_w), *([] if first else map(pin, buffers)))


def feed_call(index, place, tok, gm, held, came, gain, bias, gate_w, up_w, down_w, buffers):
    rows, width = tok.shape
    size = held.shape[0]
    hidden = gate_w.shape[0]
    first = buffers is None

    def kernel(place, tok, gm, held, came, gain, bias, gate_w, up_w, down_w, *refs):
        refs = refs if first else refs[3:]
        part, small = refs[:2]
        mix_out, unit_out, scale_out, in_all, hidden_all, grads_all = refs[2:8]
        tok_v, gm_v, held_v, came_v, weights, down_v = refs[8:14]
        mix_v, unit_v, scale_v, in_v, hidden_v, grads_v, pre, grad_hidden, back, sums, sems = refs[14:]
        here = pl.ds(index * size, size)
        load_gm = fetch(gm.at[here], gm_v, sems.at[0])
        load_down = fetch(down_w, down_v, sems.at[1])
        inputs = [
            fetch(tok.at[here], tok_v, sems.at[2]),
            fetch(held, held_v, sems.at[3]),
            fetch(came, came_v, sems.at[4]),
        ]
        load_gate = fetch(gate_w, weights.at[pl.ds(0, hidden)], sems.at[5])
        load_up = fetch(up_w, weights.at[pl.ds(hidden, hidden)], sems.at[6])
        load_gm.wait()
        load_down.wait()
        grad_hidden[...] = matmul_right(down_v[...], gm_v[...])
        for load in inputs:
            load.wait()
        take = place[0] != 0

        def norm(span):
            mix = jnp.where(take, came_v[span], held_v[span])
            mix_v[span] = mix
            unit, _, scale = norm_parts(wide(tok_v[span]) + wide(mix))
            unit_v[span] = low(unit)
            scale_v[span] = spread_lanes(scale)
            in_v[span] = low(unit * gain[1:2] + bias[1:2])

        tiles(size, norm)
        stores = [
            fetch(mix_v, mix_out, sems.at[7]),
            fetch(unit_v, unit_out, sems.at[8]),
            fetch(scale_v, scale_out, sems.at[9]),
            fetch(in_v, in_all.at[here], sems.at[10]),
        ]
        load_gate.wait()
        load_up.wait()
        pre[...] = matmul_right(weights[...], in_v[...])
        slope, cubic = 0.7978845608028654, 0.044715

        def gate(span):
            other = pl.ds(span.start + hidden, span.size)
            u, w, gz = pre[span], pre[other], grad_hidden[span]
            square = u * u
            tanh = jnp.tanh(slope * u * (1.0 + cubic * square))
            half = 0.5 * (1.0 + tanh)
            gelu = u * half
            inner = slope * (1.0 + 3.0 * cubic * square)
            gelu_grad = half + 0.5 * u * (1.0 - tanh * tanh) * inner
            hidden_v[span] = low(gelu * w)
            grads_v[span] = low(gz * w * gelu_grad)
            grads_v[other] = low(gz * gelu)

        tiles(hidden, gate, 432)
        stores.append(fetch(hidden_v, hidden_all.at[:, here], sems.at[11]))
        stores.append(fetch(grads_v, grads_all.at[:, here], sems.at[12]))
        back[...] = matmul_left(grads_v[...], weights[...])
        sums[...] = jnp.zeros_like(sums)

        def finish(span):
            piece = back[span]
            part[span] = low(piece)
            scaled = piece * wide(unit_v[span])
            sums[0:1] = sums[0:1] + jnp.sum(scaled, axis=0, keepdims=True)
            sums[1:2] = sums[1:2] + jnp.sum(piece, axis=0, keepdims=True)

        tiles(size, finish)
        small[...] = sums[0:2]
        for store in stores:
            store.wait()

    chunk = (size, width)
    return pl.pallas_call(
        kernel,
        in_specs=[SMEM] + [ANY] * 4 + [VMEM] * 2 + [ANY] * 3 + [ANY] * (0 if first else 3),
        out_specs=[VMEM] * 2 + [ANY] * 6,
        out_shape=[
            struct(chunk, jnp.bfloat16),
            in_hbm((2, width), jnp.float32),
            in_hbm(chunk),
            in_hbm(chunk),
            in_hbm((size, 128), jnp.float32),
            in_hbm((rows, width)),
            in_hbm((hidden, rows)),
            in_hbm((2 * hidden, rows)),
        ],
        scratch_shapes=[vmem(chunk)] * 4
        + [
            vmem((2 * hidden, width)),
            vmem(down_w.shape),
            vmem(chunk),
            vmem(chunk),
            vmem((size, 128), jnp.float32),
            vmem(chunk),
            vmem((hidden, size)),
            vmem((2 * hidden, size)),
            vmem((2 * hidden, size), jnp.float32),
            vmem((hidden, size), jnp.float32),
            vmem(chunk, jnp.float32),
            vmem((8, width), jnp.float32),
            pltpu.SemaphoreType.DMA((13,)),
        ],
        input_output_aliases={} if first else {10 + i: 5 + i for i in range(3)},
        compiler_params=params(40),
        cost_estimate=small_cost(),
    )(place, pin(tok), pin(gm), held, came, gain, bias, pin(gate_w), pin(up_w), pin(down_w), *([] if first else map(pin, buffers)))


def down_call(hidden, down_w):
    tall, rows = hidden.shape
    width = down_w.shape[1]
    size = rows // CHUNKS

    def kernel(hidden, down_w, *refs):
        outs, (hidden_v, down_v, product, sems) = refs[:CHUNKS], refs[CHUNKS:]
        load_hidden = fetch(hidden, hidden_v, sems.at[0])
        load_down = fetch(down_w, down_v, sems.at[1])
        load_hidden.wait()
        load_down.wait()
        stores = []
        for half in range(2):
            span = slice(half * rows // 2, (half + 1) * rows // 2)
            product[span] = low(matmul_left(hidden_v[:, span], down_v[...]))
            for i in range(half * CHUNKS // 2, (half + 1) * CHUNKS // 2):
                piece = product.at[pl.ds(i * size, size)]
                stores.append(fetch(piece, outs[i], sems.at[2 + i]))
        for store in stores:
            store.wait()

    return pl.pallas_call(
        kernel,
        in_specs=[ANY, ANY],
        out_specs=[ANY] * CHUNKS,
        out_shape=[in_hbm((size, width))] * CHUNKS,
        scratch_shapes=[
            vmem(hidden.shape),
            vmem(down_w.shape),
            vmem((rows, width)),
            pltpu.SemaphoreType.DMA((2 + CHUNKS,)),
        ],
        compiler_params=params(32),
        cost_estimate=small_cost(),
    )(pin(hidden), pin(down_w))


def gate_call(index, place, decay, gm, held, came, gain, unit, scale, output_w, gate, units, scale_ret, query, total, buffers):
    rows, width = gm.shape
    size = held.shape[0]
    values = output_w.shape[0]
    heads = values // VAL_DIM
    keys = heads * KEY_DIM
    first, last = index == 0, index == CHUNKS - 1

    def kernel(place, decay, gm, held, came, gain, unit, scale, output_w, gate, units, scale_ret, query, *refs):
        if not first:
            total_in = refs[0]
            refs = refs[4:]
        total, grad_mid, mid_all, gate_all, ret_all = refs[:5]
        gm_v, held_v, came_v, unit_v, scale_v, weight, gate_v, units_v, query_v = refs[5:14]
        mid_v, low_v, grad_v, grads_gate, ret_v, sems = refs[14:]
        here = pl.ds(index * size, size)
        inputs = [
            fetch(gm.at[here], gm_v, sems.at[0]),
            fetch(held, held_v, sems.at[1]),
            fetch(came, came_v, sems.at[2]),
            fetch(unit, unit_v, sems.at[3]),
            fetch(scale, scale_v, sems.at[4]),
        ]
        load_weight = fetch(output_w, weight, sems.at[5])
        others = [
            fetch(gate.at[:, here], gate_v, sems.at[6]),
            fetch(units.at[:, here], units_v, sems.at[7]),
            fetch(query.at[here], query_v, sems.at[8]),
        ]
        for load in inputs:
            load.wait()
        take = place[0] != 0

        def norm(span):
            gc = wide(jnp.where(take, came_v[span], held_v[span])) * gain[1:2]
            mid = wide(gm_v[span]) + norm_back(gc, wide(unit_v[span]), scale_v[span][:, 0:1])
            mid_v[span] = mid
            low_v[span] = low(mid)

        tiles(size, norm)
        stores = [
            fetch(mid_v, grad_mid, sems.at[9]),
            fetch(low_v, mid_all.at[here], sems.at[10]),
        ]
        load_weight.wait()
        grad_v[...] = matmul_right(weight[...], low_v[...])
        for load in others:
            load.wait()
        for head in range(heads):
            span = pl.ds(head * VAL_DIM, VAL_DIM)
            gy, g, o = grad_v[span], wide(gate_v[span]), wide(units_v[span])
            s = jax.nn.sigmoid(g)
            grads_gate[span] = low(gy * o * (s * (1.0 + g * (1.0 - s))))
            grad = gy * (g * s)
            mean = jnp.mean(grad, axis=0, keepdims=True)
            along = jnp.mean(grad * o, axis=0, keepdims=True)
            ret_v[span] = low(scale_ret[head][0:1] * (grad - mean - o * along))
        stores.append(fetch(grads_gate, gate_all.at[:, here], sems.at[11]))
        stores.append(fetch(ret_v, ret_all.at[:, here], sems.at[12]))
        for head in range(heads):
            q = wide(query_v[:, head * KEY_DIM : (head + 1) * KEY_DIM])
            scaled = low(q * decay_rows(decay[head], index * size + 1.0, size, 1.0))
            own = matmul(ret_v[head * VAL_DIM : (head + 1) * VAL_DIM], scaled)
            if not first:
                own = own + total_in[head]
            total[head] = low(own) if last else own
        for store in stores:
            store.wait()

    chunk = (size, width)
    extra = [] if first else [total, *map(pin, buffers)]
    return pl.pallas_call(
        kernel,
        in_specs=[SMEM, SMEM, ANY, ANY, ANY, VMEM, ANY, ANY, ANY, ANY, ANY, VMEM, ANY]
        + ([] if first else [VMEM] + [ANY] * 3),
        out_specs=[VMEM] + [ANY] * 4,
        out_shape=[
            struct((heads, VAL_DIM, KEY_DIM), jnp.bfloat16 if last else jnp.float32),
            in_hbm(chunk, jnp.float32),
            in_hbm((rows, width)),
            in_hbm((values, rows)),
            in_hbm((values, rows)),
        ],
        scratch_shapes=[vmem(chunk)] * 4
        + [
            vmem((size, 128), jnp.float32),
            vmem(output_w.shape),
            vmem((values, size)),
            vmem((values, size)),
            vmem((size, keys)),
            vmem(chunk, jnp.float32),
            vmem(chunk),
            vmem((values, size), jnp.float32),
            vmem((values, size)),
            vmem((values, size)),
            pltpu.SemaphoreType.DMA((13,)),
        ],
        input_output_aliases={} if first else {14 + i: 2 + i for i in range(3)},
        compiler_params=params(28),
        cost_estimate=small_cost(),
    )(
        place,
        decay,
        pin(gm),
        held,
        came,
        gain,
        pin(unit),
        pin(scale),
        pin(output_w),
        pin(gate),
        pin(units),
        scale_ret,
        pin(query),
        *extra,
    )


def inner_call(decay, query, key, value, grad, state, cos, sin):
    rows, keys = query.shape
    heads = keys // KEY_DIM
    size = rows // CHUNKS

    def kernel(decay, query, key, value, grad, state, cos, sin, query_grad, key_part, value_part, weights, scores):
        span = lambda i: slice(i * size, (i + 1) * size)
        rate = decay[pl.program_id(0)]
        tables = [decay_square(rate, d * size, size) for d in range(CHUNKS)]
        for i in range(CHUNKS):
            q, go = query[span(i)], grad[:, span(i)]
            for j in range(i + 1):
                weights[span(i), span(j)] = low(matmul_right(q, key[span(j)]) * tables[i - j])
                scores[span(i), span(j)] = low(
                    matmul_left(go, value[:, span(j)]) * tables[i - j]
                )
            gq = decay_rows(rate, i * size + 1.0, size, 1.0) * matmul_left(go, state[0])
            gq = gq + matmul(scores[span(i), : (i + 1) * size], key[: (i + 1) * size])
            gq = turn(gq, cos[span(i)], -sin[span(i)]) * (1.0 / KEY_DIM**0.5)
            query_grad[span(i)] = low(gq)
        for j in range(CHUNKS):
            key_part[span(j)] = matmul_left(scores[j * size :, span(j)], query[j * size :])
            value_part[:, span(j)] = matmul(grad[:, j * size :], weights[j * size :, span(j)])

    column = pl.BlockSpec((rows, KEY_DIM), lambda h: (0, h))
    per_head = pl.BlockSpec((VAL_DIM, rows), lambda h: (h, 0))
    whole = lambda a: pl.BlockSpec(a.shape, lambda h: (0,) * a.ndim)
    return pl.pallas_call(
        kernel,
        grid=(heads,),
        in_specs=[
            SMEM,
            column,
            column,
            per_head,
            per_head,
            pl.BlockSpec((1, VAL_DIM, KEY_DIM), lambda h: (h, 0, 0)),
            whole(cos),
            whole(sin),
        ],
        out_specs=[column, column, per_head],
        out_shape=[
            in_hbm((rows, 2 * keys)),
            in_hbm((rows, keys), jnp.float32),
            in_hbm((heads * VAL_DIM, rows), jnp.float32),
        ],
        scratch_shapes=[vmem((rows, rows)), vmem((rows, rows))],
        compiler_params=params(44),
        cost_estimate=small_cost(),
    )(decay, pin(query), pin(key), pin(value), pin(grad), state, cos, sin)


def back_call(index, decay, tok, mean, scale, key, value, key_part, value_part, state, cos, sin, turned, gate_grad, weights, value_all, sums_before, sums_two):
    rows, width = tok.shape
    query_w, key_w, value_w, gate_w = weights
    keys, values = key_w.shape[1], value_w.shape[0]
    heads = keys // KEY_DIM
    size = 2 * rows // CHUNKS
    half = size // 2
    first = value_all is None
    last = size * (index + 1) == rows
    extra = EXTRA_ROWS if last else 0

    def kernel(decay, tok, mean, scale, key, value, key_part, value_part, state, cos, sin, gate_grad, query_w, key_w, value_w, gate_w, turned_in, *refs):
        refs = refs if first else refs[1:]
        before, refs = (refs[0], refs[1:]) if not first else (None, refs)
        two, refs = (refs[:CHUNKS], refs[CHUNKS:]) if last else ((), refs)
        part, other_part, small, turned_all, value_all = refs[:5]
        tok_v, mean_v, scale_v, key_v, value_v, key_p, value_p, turned_v, wide_v = refs[5:14]
        narrow_w, wide_w, total, sems = refs[14:]
        here = pl.ds(index * size, size)
        loads = [
            fetch(key_part.at[here], key_p, sems.at[0]),
            fetch(value_part.at[:, here], value_p, sems.at[1]),
            fetch(key.at[here], key_v, sems.at[2]),
            fetch(value.at[:, here], value_v, sems.at[3]),
        ]
        others = [
            fetch(turned_in.at[here, pl.ds(0, keys)], turned_v.at[:, pl.ds(0, keys)], sems.at[4]),
            fetch(gate_grad.at[:, here], wide_v.at[pl.ds(values, values)], sems.at[5]),
            fetch(query_w, narrow_w.at[:, pl.ds(0, keys)], sems.at[6]),
            fetch(key_w, narrow_w.at[:, pl.ds(keys, keys)], sems.at[7]),
            fetch(value_w, wide_w.at[pl.ds(0, values)], sems.at[8]),
            fetch(gate_w, wide_w.at[pl.ds(values, values)], sems.at[9]),
        ]
        norms = [
            fetch(tok.at[here], tok_v, sems.at[10]),
            fetch(mean.at[here], mean_v, sems.at[11]),
            fetch(scale.at[here], scale_v, sems.at[12]),
        ]
        for load in loads:
            load.wait()
        for head in range(heads):
            span = slice(head * KEY_DIM, (head + 1) * KEY_DIM)
            tall = slice(head * VAL_DIM, (head + 1) * VAL_DIM)
            scaling = decay_rows(decay[head], rows - 1.0 - index * size, size, -1.0)
            gk = key_p[:, span] + scaling * matmul_left(value_v[tall], state[head])
            turned_v[:, keys + span.start : keys + span.stop] = low(turn(gk, cos[...], -sin[...]))
            scaled = low(wide(key_v[:, span]) * scaling)
            wide_v[tall] = low(value_p[tall] + matmul_right(state[head], scaled))
        stores = [
            fetch(turned_v.at[:, pl.ds(keys, keys)], turned_all.at[here, pl.ds(keys, keys)], sems.at[13]),
            fetch(wide_v.at[pl.ds(0, values)], value_all.at[:, here], sems.at[14]),
        ]
        for load in others:
            load.wait()
        total[...] = matmul_right(turned_v[...], narrow_w[...]) + matmul_left(wide_v[...], wide_w[...])
        for load in norms:
            load.wait()
        gain, bias = jnp.zeros((1, width), jnp.float32), jnp.zeros((1, width), jnp.float32)
        if not first:
            gain, bias = before[0:1], before[1:2]
        for start in range(0, size, half):
            span = pl.ds(start, half)
            piece = total[span]
            if start:
                other_part[...] = low(piece)
            else:
                part[0:half] = low(piece)
            unit = (wide(tok_v[span]) - mean_v[span][:, 0:1]) * scale_v[span][:, 0:1]
            gain = gain + jnp.sum(piece * unit, axis=0, keepdims=True)
            bias = bias + jnp.sum(piece, axis=0, keepdims=True)
        small[0:1] = gain
        small[1:2] = bias
        if last:
            sums = sum(values[...] for values in two)
            fill = jnp.zeros((extra - 4, width), jnp.float32)
            part[half : half + extra] = low(jnp.concatenate([gain, bias, sums, fill], axis=0))
        for store in stores:
            store.wait()

    row = lambda cols: pl.BlockSpec((size, cols), lambda i: (index, 0))
    whole = lambda a: pl.BlockSpec(a.shape, lambda i: (0,) * len(a.shape))
    out_shape = [
        struct((half + extra, width), jnp.bfloat16),
        struct((half, width), jnp.bfloat16),
        struct((2, width), jnp.float32),
        in_hbm((rows, 2 * keys)),
        in_hbm((values, rows)),
    ]
    tail = [] if first else [pin(value_all), sums_before]
    tail += sums_two if last else []
    return pl.pallas_call(
        kernel,
        grid=(1,),
        in_specs=[SMEM]
        + [ANY] * 7
        + [whole(state), row(128), row(128)]
        + [ANY] * 6
        + ([] if first else [ANY, whole(sums_before)])
        + ([whole(sums_two[0])] * CHUNKS if last else []),
        out_specs=[whole(shape) for shape in out_shape[:3]] + [ANY, ANY],
        out_shape=out_shape,
        scratch_shapes=[
            vmem((size, width)),
            vmem((size, 128), jnp.float32),
            vmem((size, 128), jnp.float32),
            vmem((size, keys)),
            vmem((values, size)),
            vmem((size, keys), jnp.float32),
            vmem((values, size), jnp.float32),
            vmem((size, 2 * keys)),
            vmem((2 * values, size)),
            vmem((width, 2 * keys)),
            vmem((2 * values, width)),
            vmem((size, width), jnp.float32),
            pltpu.SemaphoreType.DMA((15,)),
        ],
        input_output_aliases={16: 3} if first else {16: 3, 17: 4},
        compiler_params=params(44),
        cost_estimate=small_cost(),
    )(
        decay,
        pin(tok),
        pin(mean),
        pin(scale),
        pin(key),
        pin(value),
        pin(key_part),
        pin(value_part),
        state,
        cos,
        sin,
        pin(gate_grad),
        *map(pin, weights),
        pin(turned),
        *tail,
    )


def tokens_call(index, place, held, came, tok, mean, scale, gain, grad_mid, out):
    rows, width = tok.shape
    size = rows // CHUNKS
    piece = size // 2

    def kernel(place, held, came, tok, mean, scale, gain, grad_mid, *refs):
        def body(span):
            ga = wide(jnp.where(place[0] != 0, came[span], held[span]))
            factor = scale[span][:, 0:1]
            unit = (wide(tok[span]) - mean[span][:, 0:1]) * factor
            refs[-1][span] = grad_mid[span] + norm_back(ga * gain[0:1], unit, factor)

        tiles(piece, body)

    row = lambda cols: pl.BlockSpec((piece, cols), lambda i: (2 * index + i, 0))
    chunk = pl.BlockSpec((piece, width), lambda i: (i, 0))
    first = out is None
    return pl.pallas_call(
        kernel,
        grid=(2,),
        in_specs=[SMEM, chunk, chunk, row(width), row(128), row(128)]
        + [pl.BlockSpec(gain.shape, lambda i: (0, 0)), chunk]
        + [ANY] * (not first),
        out_specs=row(width),
        out_shape=in_hbm((rows, width), jnp.float32),
        input_output_aliases={} if first else {8: 0},
        compiler_params=params(12),
        cost_estimate=small_cost(),
    )(place, held, came, pin(tok), pin(mean), pin(scale), gain, pin(grad_mid), *([] if first else [pin(out)]))


def result_call(index, place, held, came, tok, mix, out):
    rows, width = tok.shape
    size = held.shape[0]
    piece = size // 2

    def kernel(place, held, came, tok, mix, *refs):
        total = wide(jnp.where(place[0] != 0, came[...], held[...]))
        refs[-1][...] = low(wide(tok[...]) + wide(mix[...]) + total)

    row = pl.BlockSpec((piece, width), lambda i: (2 * index + i, 0))
    chunk = pl.BlockSpec((piece, width), lambda i: (i, 0))
    first = out is None
    return pl.pallas_call(
        kernel,
        grid=(2,),
        in_specs=[SMEM, chunk, chunk, row, chunk] + [ANY] * (not first),
        out_specs=row,
        out_shape=in_hbm((rows, width)),
        input_output_aliases={} if first else {5: 0},
        compiler_params=params(8),
        cost_estimate=small_cost(),
    )(place, held, came, pin(tok), pin(mix), *([] if first else [pin(out)]))


def product_call(pairs, tall):
    rows, cols = pairs[0][1].shape
    parts = 4
    block = cols // parts
    spans, at = [], 0
    for left, _ in pairs:
        spans.append((at, at + left.shape[0] // tall))
        at = spans[-1][1]

    def kernel(*refs):
        i = pl.program_id(0)
        for n, (begin, end) in enumerate(spans):

            @pl.when((i >= begin) & (i < end))
            def _():
                refs[-1][...] = low(matmul(refs[2 * n][...], refs[2 * n + 1][...]))

    specs = []
    for begin, end in spans:

        def left_map(i, j, begin=begin, end=end):
            return (jnp.clip(i - begin, 0, end - begin - 1), 0)

        def right_map(i, j, begin=begin, end=end):
            return (0, jnp.where(i < begin, 0, jnp.where(i < end, j, parts - 1)))

        specs += [pl.BlockSpec((tall, rows), left_map), pl.BlockSpec((rows, block), right_map)]

    return pl.pallas_call(
        kernel,
        grid=(at, parts),
        in_specs=specs,
        out_specs=pl.BlockSpec((tall, block), lambda i, j: (i, j)),
        out_shape=in_hbm((at * tall, cols)),
        compiler_params=params(36),
        cost_estimate=small_cost(),
    )(*[pin(values) for pair in pairs for values in pair])


def product_rows_call(left, right):
    rows, cols = left.shape
    wide_cols = right.shape[1]
    block = cols // 4

    def kernel(left, right, out):
        out[...] = low(matmul_left(left[...], right[...]))

    return pl.pallas_call(
        kernel,
        grid=(4,),
        in_specs=[
            pl.BlockSpec((rows, block), lambda j: (0, j)),
            pl.BlockSpec((rows, wide_cols), lambda j: (0, 0), pipeline_mode=pl.Buffered(1)),
        ],
        out_specs=pl.BlockSpec((block, wide_cols), lambda j: (j, 0)),
        out_shape=in_hbm((cols, wide_cols)),
        compiler_params=params(32),
        cost_estimate=small_cost(),
    )(pin(left), pin(right))


def combine_call(groups, axis, dtype, cuts=1):
    arrays = []
    for group in groups:
        for values, _, _ in group:
            if not any(values is a for a in arrays):
                arrays.append(values)
    runs = [
        [([a is values for a in arrays].index(True), start, stop) for values, start, stop in group]
        for group in groups
    ]
    long = sum(stop - start for _, start, stop in runs[0])
    shape = list(arrays[0].shape)
    shape[axis] = long
    piece = list(shape)
    piece[1 - axis] //= cuts
    count = sum(len(group) for group in runs)

    def along(ref, start, size):
        return ref.at[pl.ds(start, size)] if axis == 0 else ref.at[:, pl.ds(start, size)]

    def kernel(*refs):
        sources, outs = refs[: len(arrays)], refs[len(arrays) : len(arrays) + cuts]
        held, sems = refs[len(arrays) + cuts : -1], refs[-1]
        loads = []
        for group, target in zip(runs, held):
            at = 0
            for which, start, stop in group:
                source = along(sources[which], start, stop - start)
                copy = fetch(source, along(target, at, stop - start), sems.at[len(loads)])
                loads.append(copy)
                at += stop - start
        for load in loads:
            load.wait()
        total = wide(held[0][...])
        for values in held[1:]:
            total = total + wide(values[...])
        total = total.astype(dtype)
        for i, out in enumerate(outs):
            size = piece[1 - axis]
            out[...] = total[:, i * size : (i + 1) * size] if axis == 0 else total[i * size : (i + 1) * size]

    made = pl.pallas_call(
        kernel,
        in_specs=[ANY] * len(arrays),
        out_specs=[VMEM] * cuts,
        out_shape=[struct(piece, dtype)] * cuts,
        scratch_shapes=[vmem(shape)] * len(runs) + [pltpu.SemaphoreType.DMA((count,))],
        compiler_params=params(16),
        cost_estimate=small_cost(),
    )(*arrays)
    return made[0] if cuts == 1 else made


class Node:
    def __init__(self, fn, deps, cost, rank, link):
        self.fn, self.cost, self.rank, self.link = fn, cost, rank, link
        self.wanted = [dep if isinstance(dep, tuple) else (dep,) for dep in deps]
        self.deps = [dep[0] for dep in self.wanted]
        self.value = None
        self.ready = None
        self.after = []

    def given(self):
        return [
            {name: node.value[name] for name in names} if names else node.value
            for node, *names in self.wanted
        ]


class Plan:
    def __init__(self):
        self.nodes = []

    def work(self, fn, deps, cost, rank):
        self.nodes.append(Node(fn, deps, cost, rank, None))
        return self.nodes[-1]

    def move(self, fn, deps, cost, link, rank=0):
        self.nodes.append(Node(fn, deps, cost, rank, link))
        return self.nodes[-1]

    def run(self):
        now, token, free, flying = 0.0, None, {}, []
        left = list(self.nodes)
        while left:
            known = [n for n in left if all(d.ready is not None for d in n.deps + n.after)]
            views = [n for n in known if n.link == "view"]
            moves = [n for n in known if n.link not in (None, "view")]
            able = [n for n in known if n.link is None]
            calls = [n for n in moves if n.link in CALLS]
            moves = [
                n
                for n in sorted(moves, key=lambda n: n.rank)
                if n.link not in CALLS
                and free.get(n.link, 0.0) - now <= QUEUE_TIME
                and len(flying) < FLYING
            ]
            fresh = all(now - f.issued <= FRESH_TIME or f.rank == SLACK for f in flying)
            if calls and (fresh and not moves or not (able or moves)):
                moves = calls
            if views or moves:
                node = (views or moves)[0]
                given = node.given()
                if token is not None and (node.link != "view" or len(given) > 1):
                    given, _ = lax.optimization_barrier((given, token))
                node.value = node.fn(*given)
                node.ready = max(d.ready for d in node.deps)
                left.remove(node)
                if node.link != "view":
                    node.ready = max(node.ready, now, free.get(node.link, 0.0)) + node.cost
                    free[node.link] = node.ready
                    now += START_COST
                    node.issued = now
                    if node.link not in CALLS:
                        flying.append(node)
                continue
            if not able:
                now += 1.0
                continue
            when = {id(n): max([d.ready for d in n.deps] + [0.0]) for n in able}
            oldest = {}
            for n in able:
                started = [d.issued for d in n.deps if d in flying]
                oldest[id(n)] = min(started) if started else None
            at_hand = [n for n in able if when[id(n)] <= now]
            arrived = [n for n in at_hand if oldest[id(n)] is not None]
            if arrived:
                next_in_order = min(arrived, key=lambda n: oldest[id(n)])
                at_hand = [n for n in at_hand if n not in arrived or n is next_in_order]
            if at_hand:
                node = min(at_hand, key=lambda n: n.rank)
            else:
                soon = [when[id(n)] for n in able]
                waiting = [
                    free[n.link] - QUEUE_TIME
                    for n in known
                    if n.link in free and n.link not in CALLS and free[n.link] - now > QUEUE_TIME
                ]
                if waiting and min(waiting) < min(soon, default=1e9) and len(flying) < FLYING:
                    now = min(waiting)
                    continue
                node = min(able, key=lambda n: (when[id(n)], n.rank))
                now = when[id(node)]
            given = node.given()
            if token is not None:
                given, _ = lax.optimization_barrier((given, token))
            made = lax.optimization_barrier(node.fn(*given))
            leaves = jax.tree.leaves(made)
            token = min(leaves, key=lambda leaf: leaf.size)
            node.value = made
            now += node.cost
            node.ready = now
            left.remove(node)
            flying = [f for f in flying if f not in node.deps]


FLYING = 5
FRESH_TIME = 14.0
SLACK = 1.5
QUEUE_TIME = 6.0
CALLS = ("scatter", "gather")
START_COST = 2.0
LINK_RATE = 100e3
CORE_RATE = 300e3


def head_total(plan, part, size, rank):
    count = lax.axis_size("head")
    mid = count // 2
    cost = size * 2 / LINK_RATE + 1.5

    def permute(pairs):
        return lambda held: lax.ppermute(held, "head", pairs)

    held = part
    for step in range(mid - 1):
        pairs = [(step, step + 1), (count - 1 - step, count - 2 - step)]
        came = plan.move(permute(pairs), [held], cost, ("in", step), rank)
        held = plan.work(add_call, [held, came], 1.5, rank)
    came = plan.move(permute([(mid - 1, mid), (mid, mid - 1)]), [held], cost, "swap", rank)
    held = plan.work(add_call, [held, came], 1.5, rank)
    for step in range(mid - 1):
        pairs = [(mid - 1 - step, mid - 2 - step), (mid + step, mid + 1 + step)]
        came = plan.move(permute(pairs), [held], cost, ("out", step), rank)
        if step < mid - 2:
            held = plan.work(out_pick(step), [held, came], 2.0, rank)
    return [held, came] if mid > 1 else [held, held]


def out_pick(step):
    def pick(held, came):
        place = lax.axis_index("head")
        mid = lax.axis_size("head") // 2
        return jnp.where((place == mid - 2 - step) | (place == mid + 1 + step), came, held)

    return pick


def exchange(values, bit):
    count = lax.axis_size("seq")
    return lax.ppermute(values, "seq", [(i, i ^ bit) for i in range(count)])


def seq_bits(flip):
    count = lax.axis_size("seq")
    bits = [1 << i for i in range(count.bit_length() - 1)]
    return [bits[0]] + bits[:0:-1] if flip else bits


def halving_lists(bits, count):
    kept = [0]
    levels = []
    for bit in reversed(bits):
        sent = [block ^ bit for block in kept]
        levels.append((bit, sent))
        kept = sent + kept
    levels.reverse()
    return levels


def arrangement(count):
    bits = [1 << i for i in range(count.bit_length() - 1)]
    if count == 8:
        kept = [2, 6, 4, 0]
        return [block ^ 1 for block in kept] + kept
    order = [0]
    for bit in reversed(bits):
        order = [block ^ bit for block in order] + order
    return order


def grad_scatter(plan, arranged, other, shape, flip, rows_last, limit, rank, cuts=1):
    count = lax.axis_size("seq")
    axis = 1 if rows_last else 0
    width = shape[axis] // count
    size = shape[0] * shape[1] * 2

    def whole(values, right):
        if rows_last:
            return product_call([(right, values)], right.shape[0])
        return product_rows_call(values, right)

    def runs_of(parts, lists, wanted):
        runs = []
        for block in wanted:
            array, at = next(
                (a, blocks.index(block)) for a, blocks in zip(parts, lists) if block in blocks
            )
            if runs and runs[-1][0] is array and runs[-1][2] == at * width:
                runs[-1] = (array, runs[-1][1], (at + 1) * width)
            else:
                runs.append((array, at * width, (at + 1) * width))
        return runs

    def level(wanted, groups, last):
        def fn(*parts):
            taken, at = [], 0
            for lists in groups:
                taken.append(runs_of(parts[at : at + len(lists)], lists, wanted))
                at += len(lists)
            return combine_call(taken, axis, jnp.float32 if last else jnp.bfloat16, cuts if last else 1)

        return fn

    made = plan.work(whole, [arranged, other], size / 2 * 2 * 1024 / 750e6 + 1.0, rank)
    groups, parts = [[arrangement(count)]], [made]
    for bit, sent in halving_lists(seq_bits(flip), count):
        pieces = 2 if size * len(sent) / count > limit else 1
        lists = []
        for piece in range(pieces):
            blocks = sent[len(sent) * piece // pieces : len(sent) * (piece + 1) // pieces]
            share = size * len(blocks) / count
            given = plan.work(
                level(blocks, list(groups), False), list(parts), share / 0.8e6 + 0.7, rank
            )
            came = plan.move(
                lambda v, bit=bit: exchange(v, bit),
                [given],
                2.0 + (share / CORE_RATE if bit == 1 else share * 2 / LINK_RATE),
                ("seq", bit),
                rank,
            )
            lists.append((came, [block ^ bit for block in blocks]))
        groups.append([blocks for _, blocks in lists])
        parts += [came for came, _ in lists]
    return plan.work(level([0], list(groups), True), list(parts), 2.0, rank)


def small_total(plan, values, rank):
    def halves(bit, keep):
        def fn(values, *came):
            half = values.shape[1] // 2
            high = ((lax.axis_index("seq") & bit) != 0) == keep
            part = jnp.where(high, values[:, half:], values[:, :half])
            return part + came[0] if came else part

        return fn

    bit = lax.axis_size("seq") // 2
    while bit:
        sent = plan.work(halves(bit, False), [values], 0.7, rank)
        came = plan.move(lambda v, bit=bit: exchange(v, bit), [sent], 3.5, ("seq", bit), rank)
        values = plan.work(halves(bit, True), [values, came], 0.7, rank)
        bit //= 2
    return values


def scan_states(plan, own, shape, log_decay, rows, backward, rank):
    count = lax.axis_size("seq")
    size = shape[0] * shape[1] * shape[2] * 2

    def update(group, last):
        def fn(total, came, *before):
            place = lax.axis_index("seq")
            inside = place & (group - 1)
            later = (place & group) != 0
            if backward:
                inside = group - 1 - inside
                later = ~later
            power = lambda n: jnp.exp(n * rows * log_decay)[:, None, None]
            mine, other = wide(total), wide(came)
            state = jnp.where(later, other * power(wide(inside)), 0.0)
            if before:
                state = state + before[0]
            if last:
                return low(state)
            spread = power(float(group))
            joined = jnp.where(later, other * spread + mine, mine * spread + other)
            return dict(total=low(joined), state=state)

        return fn

    total, state, group = own, [], 1
    while group < count:
        link = ("seq", group)
        time = 2.0 + (size / CORE_RATE if group == 1 else size * 2 / LINK_RATE)
        came = plan.move(lambda v, group=group: exchange(v, group), [total], time, link, rank)
        last = group * 2 == count
        node = plan.work(update(group, last), [total, came] + state, 1.5, rank)
        if last:
            return node
        total = plan.move(lambda v: v["total"], [(node, "total")], 0.0, "view")
        state = [plan.move(lambda v: v["state"], [(node, "state")], 0.0, "view")]
        group *= 2


def rotation(rows):
    half = KEY_DIM // 2
    positions = wide(lax.axis_index("seq") * rows + jnp.arange(rows, dtype=jnp.int32))
    freqs = 1.0 / 10000.0 ** jnp.linspace(0.0, 1.0, half, dtype=jnp.float32)
    angles = positions[:, None] * freqs[None, :]
    return jnp.cos(angles), jnp.sin(angles)


FED = ("in_all", "hidden_all", "grads_all")
BACK = ("total", "grad_mid", "mid_all", "gate_all", "ret_all")
MIX = ("gated", "units")


def on_device(
    tokens,
    norm_gain,
    norm_bias,
    query_weight,
    key_weight,
    value_weight,
    gate_weight,
    output_weight,
    ffn_gate,
    ffn_up,
    ffn_down,
    grad_out,
):
    rows, width = tokens.shape
    query_w, key_w, value_w, gate_w = (
        query_weight[0],
        key_weight[0],
        value_weight[0].T,
        gate_weight[0].T,
    )
    output_w, ffn_gate_w, ffn_up_w, ffn_down_w = (
        output_weight[0],
        ffn_gate[0].T,
        ffn_up[0].T,
        ffn_down[0],
    )
    gains, biases = norm_gain[0], norm_bias[0]
    heads_here = query_w.shape[1] // KEY_DIM
    keys_here = query_w.shape[1]
    values_here = value_w.shape[0]
    hidden_here = ffn_gate_w.shape[0]
    step = rows // CHUNKS
    count = lax.axis_size("seq")
    ends = lax.axis_index("head")
    ends = (ends == 0) | (ends == lax.axis_size("head") - 1)

    head_ids = wide(lax.axis_index("head") * heads_here) + jnp.arange(heads_here, dtype=jnp.float32)
    log_decay = jnp.log1p(-jnp.exp2(-5.0 - head_ids))
    cosine, sine = rotation(rows)
    order = arrangement(count)
    relative = jnp.bitwise_xor(
        jnp.arange(count, dtype=jnp.int32), lax.axis_index("seq").astype(jnp.int32)
    )
    position = sum(jnp.where(relative == block, order.index(block), 0) for block in order)
    place = jnp.concatenate([ends.astype(jnp.int32)[None], position.astype(jnp.int32)])

    plan = Plan()

    def view(fn, *deps):
        return plan.move(fn, list(deps), 0.0, "view")

    def pick(name, node, *after):
        return view(lambda v, *_: v[name], (node, name), *[(n, name) for n in after])

    def start(tokens):
        names = ("normed", "mean", "scale", "key", "value", "own_state")
        made = first_call(log_decay, tokens, gains, biases, cosine, sine, key_w, value_w)
        return dict(zip(names, made))

    def queries(first):
        made = second_call(place, first["normed"], cosine, sine, query_w, gate_w)
        return dict(zip(("query", "gate", "arranged"), made))

    def within(first, second):
        return intra_call(log_decay, second["query"], first["key"], first["value"])

    given, grad_given = Node(None, [], 0.0, 0, None), Node(None, [], 0.0, 0, None)
    given.value, given.ready = tokens, 0.0
    grad_given.value, grad_given.ready = grad_out, 0.0
    first = plan.work(start, [given], 13.0, 0)
    state_shape = (heads_here, VAL_DIM, KEY_DIM)
    state = scan_states(
        plan, pick("own_state", first), state_shape, log_decay, rows, False, 0
    )
    second = plan.work(queries, [(first, "normed")], 12.0, 1)
    intra = plan.work(within, [(first, "key", "value"), (second, "query")], 10.0, 2)

    def mix(index):
        def fn(second, intra, state, *before):
            made = mix_call(
                index,
                log_decay,
                second["query"],
                second["gate"],
                intra,
                state,
                output_w,
                [before[0][name] for name in MIX] if before else None,
            )
            return dict(zip(("part", "scale_ret") + MIX, made))

        return fn

    def feed(index):
        def fn(held, came, *before):
            buffers = [before[0][name] for name in FED] if before else None
            made = feed_call(
                index,
                place,
                tokens,
                grad_out,
                held,
                came,
                gains,
                biases,
                ffn_gate_w,
                ffn_up_w,
                ffn_down_w,
                buffers,
            )
            return dict(zip(("part", "small", "mix", "unit", "scale") + FED, made))

        return fn

    def back_gate(index):
        def fn(fed, mixed, units, second, held, came, *before):
            total = before[0]["total"] if before else None
            buffers = [before[0][name] for name in BACK[2:]] if before else None
            made = gate_call(
                index,
                place,
                log_decay,
                grad_out,
                held,
                came,
                gains,
                fed["unit"],
                fed["scale"],
                output_w,
                second["gate"],
                units["units"],
                mixed["scale_ret"],
                second["query"],
                total,
                buffers,
            )
            return dict(zip(BACK, made))

        return fn

    chunk_bytes = step * width * 2
    mixed, fed, back, outcome, grad_tokens, outer = [], [], [], [], [], []
    for index in range(CHUNKS):
        mixed.append(plan.work(mix(index), [(second, "query", "gate"), intra, state] + [(m, *MIX) for m in mixed[-1:]], 5.0, 0))
    for index in range(CHUNKS):
        total = head_total(plan, pick("part", mixed[index]), chunk_bytes, 1)
        fed.append(plan.work(feed(index), total + [(f, *FED) for f in fed[-1:]], 13.5, 2))
    for index in range(CHUNKS):
        total = head_total(plan, pick("part", fed[index]), chunk_bytes, 1)
        back.append(
            plan.work(
                back_gate(index),
                [
                    (fed[index], "unit", "scale"),
                    (mixed[index], "scale_ret"),
                    (mixed[-1], "units"),
                    (second, "gate", "query"),
                    *total,
                    *[(b, "total", *BACK[2:]) for b in back[-1:]],
                ],
                7.0,
                3,
            )
        )

    def result(index):
        def fn(fed, held, came, *before):
            return result_call(
                index, place, held, came, tokens, fed["mix"], before[0] if before else None
            )

        return fn

    def inside(first, second, state, back):
        made = inner_call(
            log_decay,
            second["query"],
            first["key"],
            first["value"],
            back["ret_all"],
            state,
            cosine,
            sine,
        )
        return dict(zip(("turned", "key_part", "value_part"), made))

    inner = plan.work(inside, [(first, "key", "value"), (second, "query"), state, (back[-1], "ret_all")], 9.0, 2.9)
    grad_state = scan_states(
        plan, pick("total", back[-1]), state_shape, log_decay, rows, True, 2.9
    )

    def keys_values(index):
        def fn(first, inner, grad_state, last, *others):
            before = others[0] if index else None
            made = back_call(
                index,
                log_decay,
                tokens,
                first["mean"],
                first["scale"],
                first["key"],
                first["value"],
                inner["key_part"],
                inner["value_part"],
                grad_state,
                cosine,
                sine,
                before["turned"] if before else inner["turned"],
                last["gate_all"],
                (query_w, key_w, value_w, gate_w),
                before["value_grad"] if before else None,
                before["small"] if before else None,
                [other["small"] for other in others[1:]],
            )
            return dict(zip(("part", "other_part", "small", "turned", "value_grad"), made))

        return fn

    def tokens_grad(index):
        def fn(first, back, held, came, *before):
            return tokens_call(
                index,
                place,
                held,
                came,
                tokens,
                first["mean"],
                first["scale"],
                gains,
                back["grad_mid"],
                before[0] if before else None,
            )

        return fn

    for index in range(CHUNKS // 2):
        outer.append(
            plan.work(
                keys_values(index),
                [
                    (first, "mean", "scale", "key", "value"),
                    (inner, "key_part", "value_part") + (() if outer else ("turned",)),
                    grad_state,
                    (back[-1], "gate_all"),
                    *[(o, "turned", "value_grad", "small") for o in outer[-1:]],
                    *([(f, "small") for f in fed] if index == CHUNKS // 2 - 1 else []),
                ],
                15.3,
                2.8,
            )
        )
    small = None
    for index in range(CHUNKS):
        name = "other_part" if index % 2 else "part"
        total = head_total(plan, pick(name, outer[index // 2]), chunk_bytes, 1)
        if index == CHUNKS - 2:
            small = total
        grad_tokens.append(
            plan.work(
                tokens_grad(index),
                [(first, "mean", "scale"), (back[index], "grad_mid")] + total + grad_tokens[-1:],
                4.1,
                5,
            )
        )

    def stacked(pairs, tall, rank):
        blocks = sum(count for _, _, count in pairs)
        fn = lambda *v: product_call(list(zip(v[0::2], v[1::2])), tall)
        deps = [node for left, right, _ in pairs for node in (left, right)]
        return plan.work(fn, deps, blocks * tall * width * 2 / 0.6e6 + 1.0, rank)

    called = []

    def scattered(made, tall, blocks):
        done = plan.move(
            lambda v: lax.psum_scatter(v, "seq", scatter_dimension=1, tiled=True),
            [made],
            tall * blocks * width * 2 / 73e3,
            "scatter",
        )
        called.append(done)
        split = lambda v: combine_call([[(v, 0, v.shape[1])]], 1, jnp.float32, blocks)
        return plan.work(split, [done], 1.0 + blocks, 30)

    arranged = pick("arranged", second)
    ffn_products = stacked(
        [
            (pick("grads_all", fed[-1]), pick("in_all", fed[-1]), 2),
            (pick("hidden_all", fed[-1]), grad_given, 1),
        ],
        hidden_here,
        2.95,
    )
    grads_ffn = scattered(ffn_products, hidden_here, 3)
    mix_products = stacked(
        [
            (pick("gated", mixed[-1]), pick("mid_all", back[-1]), 1),
            (pick("gate_all", back[-1]), pick("normed", first), 1),
        ],
        values_here,
        2.97,
    )
    grads_mix = scattered(mix_products, values_here, 2)

    down_parts = plan.work(
        lambda hidden: down_call(hidden, ffn_down_w),
        [pick("hidden_all", fed[-1])],
        9.0,
        2.965,
    )
    for index in range(CHUNKS):
        part = view(lambda v, index=index: v[index], down_parts)
        part.after = called[:1]
        total = head_total(plan, part, chunk_bytes, 1.5)
        outcome.append(plan.work(
                result(index), [(fed[index], "mix")] + total + outcome[-1:], 2.7, 3.3
            ))

    grad_turned = grad_scatter(
        plan, arranged, pick("turned", outer[-1]), (width, 2 * keys_here), False, False, chunk_bytes, 4.5, 2
    )
    grad_value_w = grad_scatter(
        plan, arranged, pick("value_grad", outer[-1]), (values_here, width), True, True, chunk_bytes, 4.6
    )
    def norm_sums(held, came):
        rows_small = jnp.where(ends, came, held) if lax.axis_size("head") > 2 else held
        return wide(rows_small[step : step + 4])

    small = small_total(plan, plan.work(norm_sums, small, 1.0, 4.8), 4.8)
    plan.run()
    small = small.value
    return (
        outcome[-1].value,
        grad_tokens[-1].value,
        small[0::2][None],
        small[1::2][None],
        grad_turned.value[0][None],
        grad_turned.value[1][None],
        grad_value_w.value.T[None],
        grads_mix.value[1].T[None],
        grads_mix.value[0][None],
        grads_ffn.value[0].T[None],
        grads_ffn.value[1].T[None],
        grads_ffn.value[2][None],
    )


def solution(mesh):
    return jax.shard_map(
        on_device,
        mesh=mesh,
        in_specs=(
            P("seq", None),
            P(),
            P(),
            P(None, None, "head"),
            P(None, None, "head"),
            P(None, None, "head"),
            P(None, None, "head"),
            P(None, "head", None),
            P(None, None, "head"),
            P(None, None, "head"),
            P(None, "head", None),
            P("seq", None),
        ),
        out_specs=(
            P("seq", None),
            P("seq", None),
            P(None, None, "seq"),
            P(None, None, "seq"),
            P(None, "seq", "head"),
            P(None, "seq", "head"),
            P(None, "seq", "head"),
            P(None, "seq", "head"),
            P(None, "head", "seq"),
            P(None, "seq", "head"),
            P(None, "seq", "head"),
            P(None, "head", "seq"),
        ),
        check_vma=False,
    )
```

time: 1370 us -> 683 us (0.50)
  waiting for transfers between devices: 937 us -> 179 us
  Pallas kernels: 0 us -> 300 us
  matrix products: 193 us -> 0 us
  starting transfers between devices: 1.78 us -> 141 us
  other arithmetic: 133 us -> 14.8 us
  local copies, waits for them, and re-layouts: 76.4 us -> 18.9 us
    psum x3 -> x0, waiting for transfers between devices: 651 us -> none  [the longest x1 293 us: forward_layer(): lax.psum(matmul(hidden_low, ffn_down_w).astype(jnp.bfloat16), 'head')]
    pallas_call x0 -> x75, Pallas kernels: none -> 300 us  [the longest x4 54.6 us: feed_call(): pl.pallas_call(kernel, in_specs=[SMEM] + [ANY] * 4 + [VMEM] * 2 + [ANY] *...]
    reduce_scatter x8 -> x2, waiting for transfers between devices: 228 us -> 0.01 us  [scattered(): lax.psum_scatter(v, 'seq', scatter_dimension=1, tiled=True)]
    dot_general x36 -> x0, matrix products: 193 us -> none  [the longest x8 63 us: matmul_right(): lax.dot_general(left, right, (((1,), (1,)), ((), ())), preferred_element_...]
    ppermute x0 -> x65, waiting for transfers between devices: none -> 179 us  [the longest x48 137 us: permute(): return lambda held: lax.ppermute(held, 'head', pairs)]
    ppermute x0 -> x65, starting transfers between devices: none -> 141 us  [the longest x48 127 us: permute(): return lambda held: lax.ppermute(held, 'head', pairs)]
    unnamed x17 -> x2, waiting for transfers between devices: 44.5 us -> 0.03 us
    reduce_sum x13 -> x0, other arithmetic: 43.8 us -> none  [the longest x5 26.1 us: layer_norm(): return centred * lax.rsqrt(spread + EPS) * gain + bias]
  transfers between devices with their start and end apart: 15 -> 67, of which waited for: 11 -> 25; matrix products, arithmetic and copies ran while one was open for 17% -> 1% of each run, Pallas kernels for 0% -> 41%
where the time goes in v1:
time: 683 us; the launch traced here: 670 us
  Pallas kernels  300 us (44%)
  waiting for transfers between devices  179 us (26%)
  starting transfers between devices  141 us (21%)
  local copies, waits for them, and re-layouts  18.9 us (3%)
  between operations  15.7 us (2%)
  other arithmetic  14.8 us (2%)
    ppermute x48, waiting for transfers between devices, permute(): return lambda held: lax.ppermute(held, 'head', pairs)  137 us
    ppermute x48, starting transfers between devices, permute(): return lambda held: lax.ppermute(held, 'head', pairs)  127 us
    pallas_call x4, Pallas kernels, feed_call(): pl.pallas_call(kernel, in_specs=[SMEM] + [ANY] * 4 + [VMEM] * 2 + [ANY] *...  54.6 us
    ppermute x17, waiting for transfers between devices, exchange(): return lax.ppermute(values, 'seq', [(i, i ^ bit) for i in range(count)])  41.8 us
    pallas_call x3, Pallas kernels, product_call(): pl.pallas_call(kernel, grid=(at, parts), in_specs=specs, out_specs=pl.Blo...  41.4 us
    pallas_call x32, Pallas kernels, add_call(): pl.pallas_call(kernel, grid=(2,), in_specs=[spec, spec], out_specs=spec,...  30.1 us
    pallas_call x2, Pallas kernels, back_call(): pl.pallas_call(kernel, grid=(1,), in_specs=[SMEM] + [ANY] * 7 + [whole(st...  29.6 us
    pallas_call x4, Pallas kernels, gate_call(): pl.pallas_call(kernel, in_specs=[SMEM, SMEM, ANY, ANY, ANY, VMEM, ANY, AN...  27.8 us
  transfers between devices with their start and end apart: 67, of which 25 were waited for; matrix products, arithmetic and copies ran while one was open for 1% of the time, Pallas kernels for 41%

profile of v1, /device:TPU:0, one launch (start us, length us, event | category | flops | bytes accessed | tf_op | source)
XLA Modules:
  0.0 669.8 jit_solution(2424399512521374548)
XLA Ops:
  10.7 13.1 %shard_map.211 = (bf16[1024,2048]{1,0:T(8,128)(2,1)}, f32[1024,128]{1,0:T(8,128)}, f32[1024,128]{1,0:T(8,128)}, bf16[1024,512]{1,0:T(8,128)(2,1)}, bf16[864,1024...) custom-call(f32[2]{0:T(128)S(1)} %get-tuple-element.1121.decay, bf16[1024,2048]{1,0:T(8,128)(2,1)} %tok.29, ...), custom_call_target="tpu_custom_call" | custom-call | bytes 1000000 | tf_op jit(solution)/shard_map/pallas_call | solution.py:179
  24.4 11.6 %shard_map.212 = (bf16[1024,512]{1,0:T(8,128)(2,1)}, bf16[864,1024]{1,0:T(8,128)(2,1)}, bf16[1024,2048]{1,0:T(8,128)(2,1)}) custom-call(s32[9]{0:T(128)S(1)} %pad_add_fusion.place, bf16[1024,2048]{1,0:T(8,128)(2,1)} %get-tuple-element.899.normed.refs_3_, f32[1024,128]{1,0:T(8,128)S(1)} %get-tuple-element.1113.cos, f32[1024,128]{1,0:T(8,128)S(1)} %get-tuple-element.1112.sin, ...), custom_call_target="tpu_custom_call" | custom-call | bytes 1000000 | tf_op jit(solution)/shard_map/pallas_call | solution.py:233
  39.0 5.5 shard_map.213.intra
  44.6 5.3 collective-permute-done.1
  53.8 10.4 %collective-permute-done.2 = bf16[2,432,256]{2,1,0:T(8,128)(2,1)S(1)} collective-permute-done((bf16[2,432,256]{2,1,0:T(8,128)(2,1)}, bf16[2,432,256]{2,1,0:T(8,128)(2,1)S(1)}, u32[]{:S(2)}, u32[]{:S(2)}) %collective-permute-start.2) | collective-permute-done | bytes 442400 | tf_op jit(solution)/shard_map/ppermute | solution.py:1124
  64.4 5.0 shard_map.214
  73.0 5.0 shard_map.215
  78.0 5.0 shard_map.216
  83.0 5.0 shard_map.217
  89.4 7.2 %collective-permute-done.3.came = bf16[256,2048]{1,0:T(8,128)(2,1)S(1)} collective-permute-done((bf16[256,2048]{1,0:T(8,128)(2,1)S(1)}, bf16[256,2048]{1,0:T(8,128)(2,1)S(1)}, u32[]{:S(2)}, u32[]{:S(2)}) %collective-permute-start.3) | collective-permute-done | bytes 1048608 | tf_op jit(solution)/shard_map/ppermute | solution.py:1096
  97.5 7.2 %collective-permute-start.9 = (bf16[256,2048]{1,0:T(8,128)(2,1)S(1)}, bf16[256,2048]{1,0:T(8,128)(2,1)S(1)}, u32[]{:S(2)}, u32[]{:S(2)}) collective-permute-start(bf16[256,2048]{1,0:T(8,128)(2,1)S(1)} %get-tuple-element.657.held), channel_id=1, source_target_pairs={{0,1},{3,2},{4,5},{7,6},{8,9},{11,10},{12,13},{15,14},{16,17},{19,... | collective-permute-start | bytes 3145736 | tf_op jit(solution)/shard_map/ppermute | solution.py:1096
  104.8 14.2 %collective-permute-done.5.came = bf16[256,2048]{1,0:T(8,128)(2,1)S(1)} collective-permute-done((bf16[256,2048]{1,0:T(8,128)(2,1)S(1)}, bf16[256,2048]{1,0:T(8,128)(2,1)S(1)}, u32[]{:S(2)}, u32[]{:S(2)}) %collective-permute-start.5) | collective-permute-done | bytes 1048608 | tf_op jit(solution)/shard_map/ppermute | solution.py:1096
  121.6 7.3 %collective-permute-start.6 = (bf16[256,2048]{1,0:T(8,128)(2,1)S(1)}, bf16[256,2048]{1,0:T(8,128)(2,1)S(1)}, u32[]{:S(2)}, u32[]{:S(2)}) collective-permute-start(bf16[256,2048]{1,0:T(8,128)(2,1)S(1)} %get-tuple-element.672.held), channel_id=1, source_target_pairs={{0,1},{3,2},{4,5},{7,6},{8,9},{11,10},{12,13},{15,14},{16,17},{19,... | collective-permute-start | bytes 3145736 | tf_op jit(solution)/shard_map/ppermute | solution.py:1096
  128.9 12.6 %collective-permute-done.9.came = bf16[256,2048]{1,0:T(8,128)(2,1)S(1)} collective-permute-done((bf16[256,2048]{1,0:T(8,128)(2,1)S(1)}, bf16[256,2048]{1,0:T(8,128)(2,1)S(1)}, u32[]{:S(2)}, u32[]{:S(2)}) %collective-permute-start.9) | collective-permute-done | bytes 1048608 | tf_op jit(solution)/shard_map/ppermute | solution.py:1096
  145.5 13.6 %shard_map.223 = (bf16[256,2048]{1,0:T(8,128)(2,1)S(1)}, f32[2,2048]{1,0:T(2,128)}, bf16[256,2048]{1,0:T(8,128)(2,1)}, bf16[256,2048]{1,0:T(8,128)(2,1)}, f32[25...) custom-call(s32[9]{0:T(128)S(1)} %pad_add_fusion.place, ...), custom_call_target="tpu_custom_call" | custom-call | bytes 1000000 | tf_op jit(solution)/shard_map/pallas_call | solution.py:427
  169.2 13.6 %shard_map.226 = (bf16[256,2048]{1,0:T(8,128)(2,1)S(1)}, f32[2,2048]{1,0:T(2,128)}, bf16[256,2048]{1,0:T(8,128)(2,1)}, bf16[256,2048]{1,0:T(8,128)(2,1)}, f32[25...) custom-call(s32[9]{0:T(128)S(1)} %pad_add_fusion.place, ...), custom_call_target="tpu_custom_call", output_to_operand_aliasing={{5}: (10, {}), {6}: (11, {}), {7}: (12, {})} | custom-call | bytes 1000000 | tf_op jit(solution)/shard_map/pallas_call | solution.py:427
  192.1 13.6 %shard_map.229 = (bf16[256,2048]{1,0:T(8,128)(2,1)S(1)}, f32[2,2048]{1,0:T(2,128)}, bf16[256,2048]{1,0:T(8,128)(2,1)}, bf16[256,2048]{1,0:T(8,128)(2,1)}, f32[25...) custom-call(s32[9]{0:T(128)S(1)} %pad_add_fusion.place, ...), custom_call_target="tpu_custom_call", output_to_operand_aliasing={{5}: (10, {}), {6}: (11, {}), {7}: (12, {})} | custom-call | bytes 1000000 | tf_op jit(solution)/shard_map/pallas_call | solution.py:427
  205.7 6.2 collective-permute-start.19
  217.2 14.0 %shard_map.232 = (bf16[256,2048]{1,0:T(8,128)(2,1)}, f32[2,2048]{1,0:T(2,128)}, bf16[256,2048]{1,0:T(8,128)(2,1)}, bf16[256,2048]{1,0:T(8,128)(2,1)}, f32[256,12...) custom-call(s32[9]{0:T(128)S(1)} %pad_add_fusion.place, ...), custom_call_target="tpu_custom_call", output_to_operand_aliasing={{5}: (10, {}), {6}: (11, {}), {7}: (12, {})} | custom-call | bytes 1000000 | tf_op jit(solution)/shard_map/pallas_call | solution.py:427
  232.6 6.2 collective-permute-start.20
  243.2 19.9 %shard_map.235 = bf16[2592,2048]{1,0:T(8,128)(2,1)} custom-call(bf16[1728,1024]{1,0:T(8,128)(2,1)} %get-tuple-element.756.refs_0_, bf16[1024,2048]{1,0:T(8,128)(2,1)} %get-tuple-element.757.refs_1_, bf16[864,1024]{1,0:T(8,128)(2,1)} %get-tuple-element.760.refs_2_.hidden, bf16[1024,2048]{1,0:T(8,128)(2,1)} %gm.15), custom_call_target="tpu_custom_call" | custom-call | bytes 1000000 | tf_op jit(solution)/shard_map/pallas_call | solution.py:891
  263.1 8.5 %shard_map.236 = (bf16[256,2048]{1,0:T(8,128)(2,1)}, bf16[256,2048]{1,0:T(8,128)(2,1)}, bf16[256,2048]{1,0:T(8,128)(2,1)}, bf16[256,2048]{1,0:T(8,128)(2,1)}) custom-call(bf16[864,1024]{1,0:T(8,128)(2,1)} %get-tuple-element.760.refs_2_.hidden, bf16[864,2048]{1,0:T(8,128)(2,1)} %bitcast.67), custom_call_target="tpu_custom_call" | custom-call | bytes 1000000 | tf_op jit(solution)/shard_map/pallas_call | solution.py:484
  271.6 6.8 %shard_map.237 = (f32[2,432,256]{2,1,0:T(8,128)S(1)}, f32[256,2048]{1,0:T(8,128)}, bf16[1024,2048]{1,0:T(8,128)(2,1)}, bf16[864,1024]{1,0:T(8,128)(2,1)}, bf16[864,1024]{1,0:T(8,128)(2,1)}) custom-call(s32[9]{0:T(128)S(1)} %pad_add_fusion.place, f32[2]{0:T(128)S(1)} %get-tuple-element.1121.decay, bf16[1024,2048]{1,0:T(8,128)(2,1)} %gm.15, ...), custom_call_target="tpu_custom_call" | custom-call | bytes 1000000 | tf_op jit(solution)/shard_map/pallas_call | solution.py:571
  282.8 7.1 %shard_map.240 = (f32[2,432,256]{2,1,0:T(8,128)S(1)}, f32[256,2048]{1,0:T(8,128)}, bf16[1024,2048]{1,0:T(8,128)(2,1)}, bf16[864,1024]{1,0:T(8,128)(2,1)}, bf16[864,1024]{1,0:T(8,128)(2,1)}) custom-call(s32[9]{0:T(128)S(1)} %pad_add_fusion.place, f32[2]{0:T(128)S(1)} %get-tuple-element.1121.decay, ...), custom_call_target="tpu_custom_call", output_to_operand_aliasing={{2}: (14, {}), {3}: (15, {}), {4}: (16, {})} | custom-call | bytes 1000000 | tf_op jit(solution)/shard_map/pallas_call | solution.py:571
  292.1 7.6 %collective-permute-start.27 = (bf16[256,2048]{1,0:T(8,128)(2,1)}, bf16[256,2048]{1,0:T(8,128)(2,1)S(1)}, u32[]{:S(2)}, u32[]{:S(2)}) collective-permute-start(bf16[256,2048]{1,0:T(8,128)(2,1)} %get-tuple-element.846.held), channel_id=1, source_target_pairs={{0,1},{3,2},{4,5},{7,6},{8,9},{11,10},{12,13},{15,14},{16,17},{19,... | collective-permute-start | bytes 3145736 | tf_op jit(solution)/shard_map/ppermute | solution.py:1096
  303.1 16.0 %collective-permute-done.26.came = bf16[256,2048]{1,0:T(8,128)(2,1)S(1)} collective-permute-done((bf16[256,2048]{1,0:T(8,128)(2,1)S(1)}, bf16[256,2048]{1,0:T(8,128)(2,1)S(1)}, u32[]{:S(2)}, u32[]{:S(2)}) %collective-permute-start.26) | collective-permute-done | bytes 1048608 | tf_op jit(solution)/shard_map/ppermute | solution.py:1096
  319.1 6.5 shard_map.242
  331.2 8.6 %collective-permute-done.25.came = bf16[256,2048]{1,0:T(8,128)(2,1)S(1)} collective-permute-done((bf16[256,2048]{1,0:T(8,128)(2,1)S(1)}, bf16[256,2048]{1,0:T(8,128)(2,1)S(1)}, u32[]{:S(2)}, u32[]{:S(2)}) %collective-permute-start.25) | collective-permute-done | bytes 1048608 | tf_op jit(solution)/shard_map/ppermute | solution.py:1096
  339.9 7.3 %shard_map.244 = (bf16[2,432,256]{2,1,0:T(8,128)(2,1)}, f32[256,2048]{1,0:T(8,128)}, bf16[1024,2048]{1,0:T(8,128)(2,1)}, bf16[864,1024]{1,0:T(8,128)(2,1)}, bf16[864,1024]{1,0:T(8,128)(2,1)}) custom-call(s32[9]{0:T(128)S(1)} %pad_add_fusion.place, f32[2]{0:T(128)S(1)} %get-tuple-element.1121.decay, ...), custom_call_target="tpu_custom_call", output_to_operand_aliasing={{2}: (14, {}), {3}: (15, {}), {4}: (16, {})} | custom-call | bytes 1000000 | tf_op jit(solution)/shard_map/pallas_call | solution.py:571
  351.4 9.0 %shard_map.247 = (bf16[1024,1024]{1,0:T(8,128)(2,1)}, f32[1024,512]{1,0:T(8,128)}, f32[864,1024]{1,0:T(8,128)}) custom-call(f32[2]{0:T(128)S(1)} %get-tuple-element.1121.decay, bf16[1024,512]{1,0:T(8,128)(2,1)} %get-tuple-element.875.query, bf16[1024,512]{1,0:T(8,128)(2,1)} %get-tuple-element.947.key, bf16[864,1024]{1,0:T(8,128)(2,1)} %get-tuple-element.948.value, ...), custom_call_target="tpu_custom_call" | custom-call | bytes 1000000 | tf_op jit(solution)/shard_map/pallas_call | solution.py:645
  363.0 13.9 %shard_map.248 = bf16[1728,2048]{1,0:T(8,128)(2,1)} custom-call(bf16[864,1024]{1,0:T(8,128)(2,1)} %get-tuple-element.896.refs_0_, bf16[1024,2048]{1,0:T(8,128)(2,1)} %get-tuple-element.897.refs_1_, bf16[864,1024]{1,0:T(8,128)(2,1)} %get-tuple-element.952.refs_2_.gate_grad, bf16[1024,2048]{1,0:T(8,128)(2,1)} %get-tuple-element.899.normed.refs_3_), custom_call_target="tpu_custom_call" | custom-call | bytes 1000000 | tf_op jit(solution)/shard_map/pallas_call | solution.py:891
  376.9 4.7 collective-permute-start.34
  384.5 6.5 collective-permute-start.31
  392.5 12.1 %collective-permute-done.34.came = bf16[256,2048]{1,0:T(8,128)(2,1)} collective-permute-done((bf16[256,2048]{1,0:T(8,128)(2,1)}, bf16[256,2048]{1,0:T(8,128)(2,1)}, u32[]{:S(2)}, u32[]{:S(2)}) %collective-permute-start.34) | collective-permute-done | bytes 1048608 | tf_op jit(solution)/shard_map/ppermute | solution.py:1096
  415.3 9.4 %collective-permute-done.31.came = bf16[256,2048]{1,0:T(8,128)(2,1)} collective-permute-done((bf16[256,2048]{1,0:T(8,128)(2,1)}, bf16[256,2048]{1,0:T(8,128)(2,1)}, u32[]{:S(2)}, u32[]{:S(2)}) %collective-permute-start.31) | collective-permute-done | bytes 1048608 | tf_op jit(solution)/shard_map/ppermute | solution.py:1096
  431.8 18.2 %collective-permute-done.38 = bf16[2,432,256]{2,1,0:T(8,128)(2,1)} collective-permute-done((bf16[2,432,256]{2,1,0:T(8,128)(2,1)}, bf16[2,432,256]{2,1,0:T(8,128)(2,1)}, u32[]{:S(2)}, u32[]{:S(2)}) %collective-permute-start.38) | collective-permute-done | bytes 442400 | tf_op jit(solution)/shard_map/ppermute | solution.py:1124
  453.2 14.5 %shard_map.254 = (bf16[256,2048]{1,0:T(8,128)(2,1)S(1)}, bf16[256,2048]{1,0:T(8,128)(2,1)S(1)}, f32[2,2048]{1,0:T(2,128)S(1)}, bf16[1024,1024]{1,0:T(8,128)(2,1)}, bf16[864,1024]{1,0:T(8,128)(2,1)}) custom-call(f32[2]{0:T(128)S(1)} %get-tuple-element.1121.decay, bf16[1024,2048]{1,0:T(8,128)(2,1)} %tok.29, ...), custom_call_target="tpu_custom_call", output_to_operand_aliasing={{3}: (16, {})} | custom-call | bytes 1000000 | tf_op jit(solution)/shard_map/pallas_call | solution.py:760
  467.7 4.8 collective-permute-start.43
  474.3 15.1 %shard_map.255 = (bf16[288,2048]{1,0:T(8,128)(2,1)S(1)}, bf16[256,2048]{1,0:T(8,128)(2,1)S(1)}, f32[2,2048]{1,0:T(2,128)}, bf16[1024,1024]{1,0:T(8,128)(2,1)}, bf16[864,1024]{1,0:T(8,128)(2,1)}) custom-call(f32[2]{0:T(128)S(1)} %get-tuple-element.1121.decay, bf16[1024,2048]{1,0:T(8,128)(2,1)} %tok.29, ...), custom_call_target="tpu_custom_call", output_to_operand_aliasing={{3}: (16, {}), {4}: (17, {})} | custom-call | bytes 1000000 | tf_op jit(solution)/shard_map/pallas_call | solution.py:760
  502.4 8.5 %shard_map.260.refs_0_ = bf16[2048,1024]{1,0:T(8,128)(2,1)} custom-call(bf16[1024,2048]{1,0:T(8,128)(2,1)} %get-tuple-element.1012.left.refs_1_, bf16[1024,1024]{1,0:T(8,128)(2,1)} %get-tuple-element.988.right), custom_call_target="tpu_custom_call" | custom-call | bytes 1000000 | tf_op jit(solution)/shard_map/pallas_call | solution.py:910
  516.1 5.8 collective-permute-done.40.came
  532.1 7.6 %shard_map.267.refs_0_ = bf16[864,2048]{1,0:T(8,128)(2,1)} custom-call(bf16[864,1024]{1,0:T(8,128)(2,1)} %get-tuple-element.1011.refs_0_, bf16[1024,2048]{1,0:T(8,128)(2,1)} %get-tuple-element.1012.left.refs_1_), custom_call_target="tpu_custom_call" | custom-call | bytes 1000000 | tf_op jit(solution)/shard_map/pallas_call | solution.py:891
  539.8 12.8 %collective-permute-done.51.came = bf16[288,2048]{1,0:T(8,128)(2,1)S(1)} collective-permute-done((bf16[288,2048]{1,0:T(8,128)(2,1)S(1)}, bf16[288,2048]{1,0:T(8,128)(2,1)S(1)}, u32[]{:S(2)}, u32[]{:S(2)}) %collective-permute-start.51) | collective-permute-done | bytes 1179680 | tf_op jit(solution)/shard_map/ppermute | solution.py:1096
  555.4 10.0 %collective-permute-start.47 = (bf16[256,2048]{1,0:T(8,128)(2,1)S(1)}, bf16[256,2048]{1,0:T(8,128)(2,1)S(1)}, u32[]{:S(2)}, u32[]{:S(2)}) collective-permute-start(bf16[256,2048]{1,0:T(8,128)(2,1)S(1)} %get-tuple-element.1030.held), channel_id=1, source_target_pairs={{0,1},{3,2},{4,5},{7,6},{8,9},{11,10},{12,13},{15,14},{16,17},{19,... | collective-permute-start | bytes 3145736 | tf_op jit(solution)/shard_map/ppermute | solution.py:1096
  574.8 9.0 %collective-permute-done.47.came = bf16[256,2048]{1,0:T(8,128)(2,1)S(1)} collective-permute-done((bf16[256,2048]{1,0:T(8,128)(2,1)S(1)}, bf16[256,2048]{1,0:T(8,128)(2,1)S(1)}, u32[]{:S(2)}, u32[]{:S(2)}) %collective-permute-start.47) | collective-permute-done | bytes 1048608 | tf_op jit(solution)/shard_map/ppermute | solution.py:1096
  613.9 8.8 %collective-permute-done.59.came = bf16[288,2048]{1,0:T(8,128)(2,1)} collective-permute-done((bf16[288,2048]{1,0:T(8,128)(2,1)}, bf16[288,2048]{1,0:T(8,128)(2,1)}, u32[]{:S(2)}, u32[]{:S(2)}) %collective-permute-start.59) | collective-permute-done | bytes 1179680 | tf_op jit(solution)/shard_map/ppermute | solution.py:1096
  636.2 6.8 %collective-permute-done.61.refs_3_ = bf16[864,256]{1,0:T(8,128)(2,1)} collective-permute-done((bf16[864,256]{1,0:T(8,128)(2,1)}, bf16[864,256]{1,0:T(8,128)(2,1)}, u32[]{:S(2)}, u32[]{:S(2)}) %collective-permute-start.61) | collective-permute-done | bytes 442400 | tf_op jit(solution)/shard_map/ppermute | solution.py:1124
  646.5 9.0 %collective-permute-done.58.came = bf16[256,2048]{1,0:T(8,128)(2,1)} collective-permute-done((bf16[256,2048]{1,0:T(8,128)(2,1)}, bf16[256,2048]{1,0:T(8,128)(2,1)}, u32[]{:S(2)}, u32[]{:S(2)}) %collective-permute-start.58) | collective-permute-done | bytes 1048608 | tf_op jit(solution)/shard_map/ppermute | solution.py:1096
  (288 shorter events, 197.9 us)
Async XLA Ops:
  7.2 577.8 %reduce-scatter.5.cloned.1.call-start = ((), (), s32[]{:S(2)}) async-start(), calls=%async_computation.3 | async-start | bytes 11943936 | tf_op jit(solution)/shard_map/reduce_scatter | solution.py:1560
  69.4 27.1 %collective-permute-start.3 = (bf16[256,2048]{1,0:T(8,128)(2,1)S(1)}, bf16[256,2048]{1,0:T(8,128)(2,1)S(1)}, u32[]{:S(2)}, u32[]{:S(2)}) collective-permute-start(bf16[256,2048]{1,0:T(8,128)(2,1)S(1)} %get-tuple-element.643.held), channel_id=1, source_target_pairs={{0,1},{3,2},{4,5},{7,6},{8,9},{11,10},{12,13},{15,14},{16,17},{19,... | collective-permute-start | bytes 3145736 | tf_op jit(solution)/shard_map/ppermute | solution.py:1096
  88.0 31.0 %collective-permute-start.5 = (bf16[256,2048]{1,0:T(8,128)(2,1)S(1)}, bf16[256,2048]{1,0:T(8,128)(2,1)S(1)}, u32[]{:S(2)}, u32[]{:S(2)}) collective-permute-start(bf16[256,2048]{1,0:T(8,128)(2,1)S(1)} %get-tuple-element.648.held), channel_id=1, source_target_pairs={{0,1},{3,2},{4,5},{7,6},{8,9},{11,10},{12,13},{15,14},{16,17},{19,... | collective-permute-start | bytes 3145736 | tf_op jit(solution)/shard_map/ppermute | solution.py:1096
  96.8 23.2 %collective-permute-start.4 = (bf16[256,2048]{1,0:T(8,128)(2,1)S(1)}, bf16[256,2048]{1,0:T(8,128)(2,1)S(1)}, u32[]{:S(2)}, u32[]{:S(2)}) collective-permute-start(bf16[256,2048]{1,0:T(8,128)(2,1)S(1)} %shard_map.218.held), channel_id=1, source_target_pairs={{1,2},{2,1},{5,6},{6,5},{9,10},{10,9},{13,14},{14,13},{17,18},{18,... | collective-permute-start | bytes 3145736 | tf_op jit(solution)/shard_map/ppermute | solution.py:1096
  97.5 43.9 %collective-permute-start.9 = (bf16[256,2048]{1,0:T(8,128)(2,1)S(1)}, bf16[256,2048]{1,0:T(8,128)(2,1)S(1)}, u32[]{:S(2)}, u32[]{:S(2)}) collective-permute-start(bf16[256,2048]{1,0:T(8,128)(2,1)S(1)} %get-tuple-element.657.held), channel_id=1, source_target_pairs={{0,1},{3,2},{4,5},{7,6},{8,9},{11,10},{12,13},{15,14},{16,17},{19,... | collective-permute-start | bytes 3145736 | tf_op jit(solution)/shard_map/ppermute | solution.py:1096
  119.3 23.4 %collective-permute-start.8 = (bf16[256,2048]{1,0:T(8,128)(2,1)S(1)}, bf16[256,2048]{1,0:T(8,128)(2,1)S(1)}, u32[]{:S(2)}, u32[]{:S(2)}) collective-permute-start(bf16[256,2048]{1,0:T(8,128)(2,1)S(1)} %shard_map.219.held), channel_id=1, source_target_pairs={{1,2},{2,1},{5,6},{6,5},{9,10},{10,9},{13,14},{14,13},{17,18},{18,... | collective-permute-start | bytes 3145736 | tf_op jit(solution)/shard_map/ppermute | solution.py:1096
  120.3 25.2 %collective-permute-start.7 = (bf16[256,2048]{1,0:T(8,128)(2,1)S(1)}, bf16[256,2048]{1,0:T(8,128)(2,1)S(1)}, u32[]{:S(2)}, u32[]{:S(2)}) collective-permute-start(bf16[256,2048]{1,0:T(8,128)(2,1)S(1)} %shard_map.220.held), channel_id=1, source_target_pairs={{1,0},{2,3},{5,4},{6,7},{9,8},{10,11},{13,12},{14,15},{17,16},{18,... | collective-permute-start | bytes 3145736 | tf_op jit(solution)/shard_map/ppermute | solution.py:1096
  121.6 40.1 %collective-permute-start.6 = (bf16[256,2048]{1,0:T(8,128)(2,1)S(1)}, bf16[256,2048]{1,0:T(8,128)(2,1)S(1)}, u32[]{:S(2)}, u32[]{:S(2)}) collective-permute-start(bf16[256,2048]{1,0:T(8,128)(2,1)S(1)} %get-tuple-element.672.held), channel_id=1, source_target_pairs={{0,1},{3,2},{4,5},{7,6},{8,9},{11,10},{12,13},{15,14},{16,17},{19,... | collective-permute-start | bytes 3145736 | tf_op jit(solution)/shard_map/ppermute | solution.py:1096
  141.8 25.5 %collective-permute-start.13 = (bf16[256,2048]{1,0:T(8,128)(2,1)S(1)}, bf16[256,2048]{1,0:T(8,128)(2,1)S(1)}, u32[]{:S(2)}, u32[]{:S(2)}) collective-permute-start(bf16[256,2048]{1,0:T(8,128)(2,1)S(1)} %shard_map.221.held), channel_id=1, source_target_pairs={{1,2},{2,1},{5,6},{6,5},{9,10},{10,9},{13,14},{14,13},{17,18},{18,... | collective-permute-start | bytes 3145736 | tf_op jit(solution)/shard_map/ppermute | solution.py:1096
  143.0 26.2 %collective-permute-start.12 = (bf16[256,2048]{1,0:T(8,128)(2,1)S(1)}, bf16[256,2048]{1,0:T(8,128)(2,1)S(1)}, u32[]{:S(2)}, u32[]{:S(2)}) collective-permute-start(bf16[256,2048]{1,0:T(8,128)(2,1)S(1)} %shard_map.222.held), channel_id=1, source_target_pairs={{1,0},{2,3},{5,4},{6,7},{9,8},{10,11},{13,12},{14,15},{17,16},{18,... | collective-permute-start | bytes 3145736 | tf_op jit(solution)/shard_map/ppermute | solution.py:1096
  161.7 26.5 %collective-permute-start.11 = (bf16[256,2048]{1,0:T(8,128)(2,1)S(1)}, bf16[256,2048]{1,0:T(8,128)(2,1)S(1)}, u32[]{:S(2)}, u32[]{:S(2)}) collective-permute-start(bf16[256,2048]{1,0:T(8,128)(2,1)S(1)} %get-tuple-element.698.held), channel_id=1, source_target_pairs={{0,1},{3,2},{4,5},{7,6},{8,9},{11,10},{12,13},{15,14},{16,17},{19,... | collective-permute-start | bytes 3145736 | tf_op jit(solution)/shard_map/ppermute | solution.py:1096
  167.5 24.6 %collective-permute-start.15 = (bf16[256,2048]{1,0:T(8,128)(2,1)S(1)}, bf16[256,2048]{1,0:T(8,128)(2,1)S(1)}, u32[]{:S(2)}, u32[]{:S(2)}) collective-permute-start(bf16[256,2048]{1,0:T(8,128)(2,1)S(1)} %shard_map.225.held), channel_id=1, source_target_pairs={{1,0},{2,3},{5,4},{6,7},{9,8},{10,11},{13,12},{14,15},{17,16},{18,... | collective-permute-start | bytes 3145736 | tf_op jit(solution)/shard_map/ppermute | solution.py:1096
  182.8 29.0 %collective-permute-start.17 = (bf16[256,2048]{1,0:T(8,128)(2,1)S(1)}, bf16[256,2048]{1,0:T(8,128)(2,1)S(1)}, u32[]{:S(2)}, u32[]{:S(2)}) collective-permute-start(bf16[256,2048]{1,0:T(8,128)(2,1)S(1)} %get-tuple-element.727.held), channel_id=1, source_target_pairs={{0,1},{3,2},{4,5},{7,6},{8,9},{11,10},{12,13},{15,14},{16,17},{19,... | collective-permute-start | bytes 3145736 | tf_op jit(solution)/shard_map/ppermute | solution.py:1096
  188.5 24.4 %collective-permute-start.16 = (bf16[256,2048]{1,0:T(8,128)(2,1)S(1)}, bf16[256,2048]{1,0:T(8,128)(2,1)S(1)}, u32[]{:S(2)}, u32[]{:S(2)}) collective-permute-start(bf16[256,2048]{1,0:T(8,128)(2,1)S(1)} %shard_map.227.held), channel_id=1, source_target_pairs={{1,2},{2,1},{5,6},{6,5},{9,10},{10,9},{13,14},{14,13},{17,18},{18,... | collective-permute-start | bytes 3145736 | tf_op jit(solution)/shard_map/ppermute | solution.py:1096
  189.5 26.2 %collective-permute-start.14 = (bf16[256,2048]{1,0:T(8,128)(2,1)S(1)}, bf16[256,2048]{1,0:T(8,128)(2,1)S(1)}, u32[]{:S(2)}, u32[]{:S(2)}) collective-permute-start(bf16[256,2048]{1,0:T(8,128)(2,1)S(1)} %shard_map.228.held), channel_id=1, source_target_pairs={{1,0},{2,3},{5,4},{6,7},{9,8},{10,11},{13,12},{14,15},{17,16},{18,... | collective-permute-start | bytes 3145736 | tf_op jit(solution)/shard_map/ppermute | solution.py:1096
  205.7 25.8 %collective-permute-start.19 = (bf16[256,2048]{1,0:T(8,128)(2,1)S(1)}, bf16[256,2048]{1,0:T(8,128)(2,1)S(1)}, u32[]{:S(2)}, u32[]{:S(2)}) collective-permute-start(bf16[256,2048]{1,0:T(8,128)(2,1)S(1)} %get-tuple-element.752.held), channel_id=1, source_target_pairs={{0,1},{3,2},{4,5},{7,6},{8,9},{11,10},{12,13},{15,14},{16,17},{19,... | collective-permute-start | bytes 3145736 | tf_op jit(solution)/shard_map/ppermute | solution.py:1096
  212.2 26.7 %collective-permute-start.18 = (bf16[256,2048]{1,0:T(8,128)(2,1)S(1)}, bf16[256,2048]{1,0:T(8,128)(2,1)S(1)}, u32[]{:S(2)}, u32[]{:S(2)}) collective-permute-start(bf16[256,2048]{1,0:T(8,128)(2,1)S(1)} %shard_map.230.held), channel_id=1, source_target_pairs={{1,2},{2,1},{5,6},{6,5},{9,10},{10,9},{13,14},{14,13},{17,18},{18,... | collective-permute-start | bytes 3145736 | tf_op jit(solution)/shard_map/ppermute | solution.py:1096
  215.7 55.8 %collective-permute-start.21 = (bf16[256,2048]{1,0:T(8,128)(2,1)S(1)}, bf16[256,2048]{1,0:T(8,128)(2,1)}, u32[]{:S(2)}, u32[]{:S(2)}) collective-permute-start(bf16[256,2048]{1,0:T(8,128)(2,1)S(1)} %shard_map.231.held), channel_id=1, source_target_pairs={{1,0},{2,3},{5,4},{6,7},{9,8},{10,11},{13,12},{14,15},{17,16},{18,... | collective-permute-start | bytes 3145736 | tf_op jit(solution)/shard_map/ppermute | solution.py:1096
  232.6 45.8 %collective-permute-start.20 = (bf16[256,2048]{1,0:T(8,128)(2,1)}, bf16[256,2048]{1,0:T(8,128)(2,1)}, u32[]{:S(2)}, u32[]{:S(2)}) collective-permute-start(bf16[256,2048]{1,0:T(8,128)(2,1)} %get-tuple-element.785.held), channel_id=1, source_target_pairs={{0,1},{3,2},{4,5},{7,6},{8,9},{11,10},{12,13},{15,14},{16,17},{19,... | collective-permute-start | bytes 3145736 | tf_op jit(solution)/shard_map/ppermute | solution.py:1096
  238.8 42.3 %collective-permute-start.24 = (bf16[256,2048]{1,0:T(8,128)(2,1)}, bf16[256,2048]{1,0:T(8,128)(2,1)}, u32[]{:S(2)}, u32[]{:S(2)}) collective-permute-start(bf16[256,2048]{1,0:T(8,128)(2,1)} %shard_map.233.held), channel_id=1, source_target_pairs={{1,2},{2,1},{5,6},{6,5},{9,10},{10,9},{13,14},{14,13},{17,18},{18,... | collective-permute-start | bytes 3145736 | tf_op jit(solution)/shard_map/ppermute | solution.py:1096
  241.5 41.3 %collective-permute-start.23 = (bf16[256,2048]{1,0:T(8,128)(2,1)}, bf16[256,2048]{1,0:T(8,128)(2,1)}, u32[]{:S(2)}, u32[]{:S(2)}) collective-permute-start(bf16[256,2048]{1,0:T(8,128)(2,1)} %shard_map.234.held), channel_id=1, source_target_pairs={{1,0},{2,3},{5,4},{6,7},{9,8},{10,11},{13,12},{14,15},{17,16},{18,... | collective-permute-start | bytes 3145736 | tf_op jit(solution)/shard_map/ppermute | solution.py:1096
  290.0 317.6 %reduce-scatter.3.cloned.1.call-start = ((), (), s32[]{:S(2)}) async-start(), calls=%async_computation.2 | async-start | bytes 7962624 | tf_op jit(solution)/shard_map/reduce_scatter | solution.py:1560
  290.8 28.3 %collective-permute-start.26 = (bf16[256,2048]{1,0:T(8,128)(2,1)S(1)}, bf16[256,2048]{1,0:T(8,128)(2,1)S(1)}, u32[]{:S(2)}, u32[]{:S(2)}) collective-permute-start(bf16[256,2048]{1,0:T(8,128)(2,1)S(1)} %shard_map.239.held), channel_id=1, source_target_pairs={{1,0},{2,3},{5,4},{6,7},{9,8},{10,11},{13,12},{14,15},{17,16},{18,... | collective-permute-start | bytes 3145736 | tf_op jit(solution)/shard_map/ppermute | solution.py:1096
  292.1 37.2 %collective-permute-start.27 = (bf16[256,2048]{1,0:T(8,128)(2,1)}, bf16[256,2048]{1,0:T(8,128)(2,1)S(1)}, u32[]{:S(2)}, u32[]{:S(2)}) collective-permute-start(bf16[256,2048]{1,0:T(8,128)(2,1)} %get-tuple-element.846.held), channel_id=1, source_target_pairs={{0,1},{3,2},{4,5},{7,6},{8,9},{11,10},{12,13},{15,14},{16,17},{19,... | collective-permute-start | bytes 3145736 | tf_op jit(solution)/shard_map/ppermute | solution.py:1096
  301.5 38.4 %collective-permute-start.25 = (bf16[256,2048]{1,0:T(8,128)(2,1)S(1)}, bf16[256,2048]{1,0:T(8,128)(2,1)S(1)}, u32[]{:S(2)}, u32[]{:S(2)}) collective-permute-start(bf16[256,2048]{1,0:T(8,128)(2,1)S(1)} %shard_map.241.held), channel_id=1, source_target_pairs={{1,0},{2,3},{5,4},{6,7},{9,8},{10,11},{13,12},{14,15},{17,16},{18,... | collective-permute-start | bytes 3145736 | tf_op jit(solution)/shard_map/ppermute | solution.py:1096
  376.9 27.7 %collective-permute-start.34 = (bf16[256,2048]{1,0:T(8,128)(2,1)}, bf16[256,2048]{1,0:T(8,128)(2,1)}, u32[]{:S(2)}, u32[]{:S(2)}) collective-permute-start(bf16[256,2048]{1,0:T(8,128)(2,1)} %get-tuple-element.900.held), channel_id=1, source_target_pairs={{0,1},{3,2},{4,5},{7,6},{8,9},{11,10},{12,13},{15,14},{16,17},{19,... | collective-permute-start | bytes 3145736 | tf_op jit(solution)/shard_map/ppermute | solution.py:1096
  381.6 26.3 %collective-permute-start.33 = (bf16[256,2048]{1,0:T(8,128)(2,1)S(1)}, bf16[256,2048]{1,0:T(8,128)(2,1)}, u32[]{:S(2)}, u32[]{:S(2)}) collective-permute-start(bf16[256,2048]{1,0:T(8,128)(2,1)S(1)} %copy-done.5), channel_id=1, source_target_pairs={{1,2},{2,1},{5,6},{6,5},{9,10},{10,9},{13,14},{14,13},{17,18},{18,... | collective-permute-start | bytes 3145736 | tf_op jit(solution)/shard_map/ppermute | solution.py:1096
  383.3 26.0 %collective-permute-start.32 = (bf16[256,2048]{1,0:T(8,128)(2,1)S(1)}, bf16[256,2048]{1,0:T(8,128)(2,1)}, u32[]{:S(2)}, u32[]{:S(2)}) collective-permute-start(bf16[256,2048]{1,0:T(8,128)(2,1)S(1)} %shard_map.246.held), channel_id=1, source_target_pairs={{1,0},{2,3},{5,4},{6,7},{9,8},{10,11},{13,12},{14,15},{17,16},{18,... | collective-permute-start | bytes 3145736 | tf_op jit(solution)/shard_map/ppermute | solution.py:1096
  384.5 40.2 %collective-permute-start.31 = (bf16[256,2048]{1,0:T(8,128)(2,1)}, bf16[256,2048]{1,0:T(8,128)(2,1)}, u32[]{:S(2)}, u32[]{:S(2)}) collective-permute-start(bf16[256,2048]{1,0:T(8,128)(2,1)} %get-tuple-element.907.held), channel_id=1, source_target_pairs={{0,1},{3,2},{4,5},{7,6},{8,9},{11,10},{12,13},{15,14},{16,17},{19,... | collective-permute-start | bytes 3145736 | tf_op jit(solution)/shard_map/ppermute | solution.py:1096
  391.1 35.1 %collective-permute-start.35 = (bf16[2,432,256]{2,1,0:T(8,128)(2,1)}, bf16[2,432,256]{2,1,0:T(8,128)(2,1)}, u32[]{:S(2)}, u32[]{:S(2)}) collective-permute-start(bf16[2,432,256]{2,1,0:T(8,128)(2,1)} %get-tuple-element.913), channel_id=1, source_target_pairs={{0,8},{4,12},{8,0},{12,4},{16,24},{20,28},{24,16},{28,20},{1,9},{5... | collective-permute-start | bytes 1327112 | tf_op jit(solution)/shard_map/ppermute | solution.py:1124
  412.3 39.2 %collective-permute-start.39 = (bf16[256,2048]{1,0:T(8,128)(2,1)}, bf16[256,2048]{1,0:T(8,128)(2,1)}, u32[]{:S(2)}, u32[]{:S(2)}) collective-permute-start(bf16[256,2048]{1,0:T(8,128)(2,1)} %shard_map.249.held), channel_id=1, source_target_pairs={{1,2},{2,1},{5,6},{6,5},{9,10},{10,9},{13,14},{14,13},{17,18},{18,... | collective-permute-start | bytes 3145736 | tf_op jit(solution)/shard_map/ppermute | solution.py:1096
  414.0 75.3 %collective-permute-start.37 = (bf16[256,2048]{1,0:T(8,128)(2,1)S(1)}, bf16[256,2048]{1,0:T(8,128)(2,1)}, u32[]{:S(2)}, u32[]{:S(2)}) collective-permute-start(bf16[256,2048]{1,0:T(8,128)(2,1)S(1)} %shard_map.250.held), channel_id=1, source_target_pairs={{1,0},{2,3},{5,4},{6,7},{9,8},{10,11},{13,12},{14,15},{17,16},{18,... | collective-permute-start | bytes 3145736 | tf_op jit(solution)/shard_map/ppermute | solution.py:1096
  428.7 68.3 %collective-permute-start.36 = (bf16[256,2048]{1,0:T(8,128)(2,1)S(1)}, bf16[256,2048]{1,0:T(8,128)(2,1)}, u32[]{:S(2)}, u32[]{:S(2)}) collective-permute-start(bf16[256,2048]{1,0:T(8,128)(2,1)S(1)} %shard_map.252.held), channel_id=1, source_target_pairs={{1,2},{2,1},{5,6},{6,5},{9,10},{10,9},{13,14},{14,13},{17,18},{18,... | collective-permute-start | bytes 3145736 | tf_op jit(solution)/shard_map/ppermute | solution.py:1096
  467.7 34.4 %collective-permute-start.43 = (bf16[256,2048]{1,0:T(8,128)(2,1)S(1)}, bf16[256,2048]{1,0:T(8,128)(2,1)S(1)}, u32[]{:S(2)}, u32[]{:S(2)}) collective-permute-start(bf16[256,2048]{1,0:T(8,128)(2,1)S(1)} %get-tuple-element.985.held), channel_id=1, source_target_pairs={{0,1},{3,2},{4,5},{7,6},{8,9},{11,10},{12,13},{15,14},{16,17},{19,... | collective-permute-start | bytes 3145736 | tf_op jit(solution)/shard_map/ppermute | solution.py:1096
  472.5 27.1 %collective-permute-start.41 = (bf16[256,2048]{1,0:T(8,128)(2,1)S(1)}, bf16[256,2048]{1,0:T(8,128)(2,1)S(1)}, u32[]{:S(2)}, u32[]{:S(2)}) collective-permute-start(bf16[256,2048]{1,0:T(8,128)(2,1)S(1)} %shard_map.253.held), channel_id=1, source_target_pairs={{1,0},{2,3},{5,4},{6,7},{9,8},{10,11},{13,12},{14,15},{17,16},{18,... | collective-permute-start | bytes 3145736 | tf_op jit(solution)/shard_map/ppermute | solution.py:1096
  489.4 25.6 %collective-permute-start.42 = (bf16[256,2048]{1,0:T(8,128)(2,1)S(1)}, bf16[256,2048]{1,0:T(8,128)(2,1)S(1)}, u32[]{:S(2)}, u32[]{:S(2)}) collective-permute-start(bf16[256,2048]{1,0:T(8,128)(2,1)S(1)} %get-tuple-element.991.held), channel_id=1, source_target_pairs={{0,1},{3,2},{4,5},{7,6},{8,9},{11,10},{12,13},{15,14},{16,17},{19,... | collective-permute-start | bytes 3145736 | tf_op jit(solution)/shard_map/ppermute | solution.py:1096
  498.3 23.6 %collective-permute-start.40 = (bf16[256,2048]{1,0:T(8,128)(2,1)S(1)}, bf16[256,2048]{1,0:T(8,128)(2,1)S(1)}, u32[]{:S(2)}, u32[]{:S(2)}) collective-permute-start(bf16[256,2048]{1,0:T(8,128)(2,1)S(1)} %shard_map.257.held), channel_id=1, source_target_pairs={{1,0},{2,3},{5,4},{6,7},{9,8},{10,11},{13,12},{14,15},{17,16},{18,... | collective-permute-start | bytes 3145736 | tf_op jit(solution)/shard_map/ppermute | solution.py:1096
  524.5 28.0 %collective-permute-start.51 = (bf16[288,2048]{1,0:T(8,128)(2,1)S(1)}, bf16[288,2048]{1,0:T(8,128)(2,1)S(1)}, u32[]{:S(2)}, u32[]{:S(2)}) collective-permute-start(bf16[288,2048]{1,0:T(8,128)(2,1)S(1)} %get-tuple-element.1016.held), channel_id=1, source_target_pairs={{0,1},{3,2},{4,5},{7,6},{8,9},{11,10},{12,13},{15,14},{16,17},{19,... | collective-permute-start | bytes 3538952 | tf_op jit(solution)/shard_map/ppermute | solution.py:1096
  527.2 38.5 %collective-permute-start.50 = (bf16[256,2048]{1,0:T(8,128)(2,1)S(1)}, bf16[256,2048]{1,0:T(8,128)(2,1)S(1)}, u32[]{:S(2)}, u32[]{:S(2)}) collective-permute-start(bf16[256,2048]{1,0:T(8,128)(2,1)S(1)} %shard_map.263.held), channel_id=1, source_target_pairs={{1,2},{2,1},{5,6},{6,5},{9,10},{10,9},{13,14},{14,13},{17,18},{18,... | collective-permute-start | bytes 3145736 | tf_op jit(solution)/shard_map/ppermute | solution.py:1096
  528.2 38.9 %collective-permute-start.49 = (bf16[256,2048]{1,0:T(8,128)(2,1)S(1)}, bf16[256,2048]{1,0:T(8,128)(2,1)S(1)}, u32[]{:S(2)}, u32[]{:S(2)}) collective-permute-start(bf16[256,2048]{1,0:T(8,128)(2,1)S(1)} %shard_map.265.held), channel_id=1, source_target_pairs={{1,0},{2,3},{5,4},{6,7},{9,8},{10,11},{13,12},{14,15},{17,16},{18,... | collective-permute-start | bytes 3145736 | tf_op jit(solution)/shard_map/ppermute | solution.py:1096
  530.0 41.3 %collective-permute-start.48 = (bf16[512,1024]{1,0:T(8,128)(2,1)S(1)}, bf16[512,1024]{1,0:T(8,128)(2,1)S(1)}, u32[]{:S(2)}, u32[]{:S(2)}) collective-permute-start(bf16[512,1024]{1,0:T(8,128)(2,1)S(1)} %shard_map.266), channel_id=1, source_target_pairs={{0,8},{4,12},{8,0},{12,4},{16,24},{20,28},{24,16},{28,20},{1,9},{5... | collective-permute-start | bytes 3145736 | tf_op jit(solution)/shard_map/ppermute | solution.py:1124
  553.7 34.3 %collective-permute-start.55 = (bf16[288,2048]{1,0:T(8,128)(2,1)}, bf16[288,2048]{1,0:T(8,128)(2,1)}, u32[]{:S(2)}, u32[]{:S(2)}) collective-permute-start(bf16[288,2048]{1,0:T(8,128)(2,1)} %shard_map.268.held), channel_id=1, source_target_pairs={{1,2},{2,1},{5,6},{6,5},{9,10},{10,9},{13,14},{14,13},{17,18},{18,... | collective-permute-start | bytes 3538952 | tf_op jit(solution)/shard_map/ppermute | solution.py:1096
  555.4 28.5 %collective-permute-start.47 = (bf16[256,2048]{1,0:T(8,128)(2,1)S(1)}, bf16[256,2048]{1,0:T(8,128)(2,1)S(1)}, u32[]{:S(2)}, u32[]{:S(2)}) collective-permute-start(bf16[256,2048]{1,0:T(8,128)(2,1)S(1)} %get-tuple-element.1030.held), channel_id=1, source_target_pairs={{0,1},{3,2},{4,5},{7,6},{8,9},{11,10},{12,13},{15,14},{16,17},{19,... | collective-permute-start | bytes 3145736 | tf_op jit(solution)/shard_map/ppermute | solution.py:1096
  573.6 27.4 %collective-permute-start.57 = (bf16[256,2048]{1,0:T(8,128)(2,1)}, bf16[256,2048]{1,0:T(8,128)(2,1)}, u32[]{:S(2)}, u32[]{:S(2)}) collective-permute-start(bf16[256,2048]{1,0:T(8,128)(2,1)} %shard_map.270.held), channel_id=1, source_target_pairs={{1,0},{2,3},{5,4},{6,7},{9,8},{10,11},{13,12},{14,15},{17,16},{18,... | collective-permute-start | bytes 3145736 | tf_op jit(solution)/shard_map/ppermute | solution.py:1096
  591.1 31.7 %collective-permute-start.59 = (bf16[288,2048]{1,0:T(8,128)(2,1)}, bf16[288,2048]{1,0:T(8,128)(2,1)}, u32[]{:S(2)}, u32[]{:S(2)}) collective-permute-start(bf16[288,2048]{1,0:T(8,128)(2,1)} %shard_map.276.held), channel_id=1, source_target_pairs={{1,0},{2,3},{5,4},{6,7},{9,8},{10,11},{13,12},{14,15},{17,16},{18,... | collective-permute-start | bytes 3538952 | tf_op jit(solution)/shard_map/ppermute | solution.py:1096
  607.4 22.5 %collective-permute-start.60 = (bf16[864,512]{1,0:T(8,128)(2,1)}, bf16[864,512]{1,0:T(8,128)(2,1)}, u32[]{:S(2)}, u32[]{:S(2)}) collective-permute-start(bf16[864,512]{1,0:T(8,128)(2,1)} %shard_map.279), channel_id=1, source_target_pairs={{0,16},{4,20},{8,24},{12,28},{16,0},{20,4},{24,8},{28,12},{1,17},{... | collective-permute-start | bytes 2654216 | tf_op jit(solution)/shard_map/ppermute | solution.py:1124
  612.6 42.9 %collective-permute-start.58 = (bf16[256,2048]{1,0:T(8,128)(2,1)}, bf16[256,2048]{1,0:T(8,128)(2,1)}, u32[]{:S(2)}, u32[]{:S(2)}) collective-permute-start(bf16[256,2048]{1,0:T(8,128)(2,1)} %shard_map.281.held), channel_id=1, source_target_pairs={{1,0},{2,3},{5,4},{6,7},{9,8},{10,11},{13,12},{14,15},{17,16},{18,... | collective-permute-start | bytes 3145736 | tf_op jit(solution)/shard_map/ppermute | solution.py:1096
  636.1 23.5 %collective-permute-start.63 = (f32[4,512]{1,0:T(4,128)}, f32[4,512]{1,0:T(4,128)}, u32[]{:S(2)}, u32[]{:S(2)}) collective-permute-start(f32[4,512]{1,0:T(4,128)} %slice_select_fusion.2), channel_id=1, source_target_pairs={{0,8},{4,12},{8,0},{12,4},{16,24},{20,28},{24,16},{28,20},{1,9},{5... | collective-permute-start | bytes 24584 | tf_op jit(solution)/shard_map/ppermute | solution.py:1124
  (69 other events, 1161.2 us)
Sparse Core Ops, SparseCore 0:
  290.1 83.6 reduce-scatter.4
  377.3 73.6 reduce-scatter.2
